TPU v7x, 256 devices: a whole 4x4x8 slice. The times are simulated.
256 devices in a mesh: ctx: 64 (over z, x_hi, y), head: 4 (over x_lo, core).
Axes of the slice: x: 4 (x_hi: 2, x_lo: 2; x = x_hi * 2 + x_lo), y: 4, z: 8, core: 2. Of those that a mesh axis runs over, the one named last changes fastest.
Arguments:
- queries: bfloat16 [32768, 8192], P(('ctx', 'head')), may hold values from -80 to 80
- key_vectors: bfloat16 [32768, 1024], P(('ctx', 'head')), may hold values from -4 to 4
- value_vectors: bfloat16 [32768, 1024], P(('ctx', 'head')), may hold values from -6 to 6
- out_grad: bfloat16 [32768, 8192], P(('ctx', 'head')), may hold values from -6 to 6
- doc_starts: int32 [127], replicated, may hold values from 2 to 32766, as said below
Outputs:
- grad_query: bfloat16 [32768, 8192], P(('ctx', 'head'))
- grad_key: bfloat16 [32768, 1024], P(('ctx', 'head'))
- grad_value: bfloat16 [32768, 1024], P(('ctx', 'head'))
Inputs may be any that keep to these rules, and one draw needn't show every extreme that they name: `doc_starts`: increasing and even; every document, the first and last too, holds at most 510 tokens, and one holds exactly 510.
All inputs are finite; a program needn't handle non-finite values.
Results may differ from a plain program's by a relative error of at most 0.012.
Values may be sent and summed in bfloat16 or wider, within the bound.
No kernel may reach another device: no remote copies, remote signals or barrier semaphores. Data moves between devices by JAX's collectives and lax.ppermute only.
A program may use at most 192 MiB of HBM per device.

v0:
```python
import functools, math
import jax, jax.numpy as jnp
from jax import lax
from jax.experimental import pallas as pl
from jax.experimental.pallas import tpu as pltpu
from jax.sharding import PartitionSpec as P
HD=128; BLK=128; GRP=8; WIN=640
SCALE=1.0/math.sqrt(HD); LOG2E=1.4426950408889634
TT=(((1,),(1,)),((),()))
NN=(((1,),(0,)),((),()))
TN=(((0,),(0,)),((),()))
f32=jnp.float32; bf16=jnp.bfloat16

def kernel(scal, first_ref, qa, qb, ga, gb, y_ref, x_ref, o_ref, *rest, pair, mode):
    dqa, dqb, dy, dx, do, kv, bias, pt, dst, acc = rest[-10:]
    j = pl.program_id(0)
    off_a = pl.multiple_of(scal[1]*BLK, BLK)
    off_b = pl.multiple_of((1-scal[1])*BLK, BLK)
    kv[0:256] = y_ref[...]; kv[256:512]=x_ref[...]; kv[512:768]=o_ref[...]
    @pl.when(j==0)
    def _():
        for s, off in ((0,off_a),(1,off_b)):
            t = lax.broadcasted_iota(jnp.int32,(WIN,BLK),0)+off
            p = lax.broadcasted_iota(jnp.int32,(WIN,BLK),1)+off+512
            ok = (t<=p)&(t>=first_ref[s:s+1,:])
            bias[s]=jnp.where(ok,0.0,-1e30).astype(f32)
    acc[...]=jnp.zeros_like(acc)
    for s,(q,g,dq,off) in enumerate(((qa,ga,dqa,off_a),(qb,gb,dqb,off_b))):
        K=kv[pl.ds(off,WIN),0:128]; V=kv[pl.ds(off,WIN),128:256]
        KT=K.T
        for i in range(0,GRP,pair):
            cols=[slice((i+u)*HD,(i+u+1)*HD) for u in range(pair)]
            Q=jnp.concatenate([q[:,c] for c in cols],axis=0)
            G=jnp.concatenate([g[:,c] for c in cols],axis=0)
            S=lax.dot_general(K,Q,TT,preferred_element_type=f32)
            D=lax.dot_general(V,G,TT,preferred_element_type=f32)
            b=bias[s]
            b=jnp.concatenate([b]*pair,axis=1)
            u=S*(SCALE*LOG2E)+b
            m=jnp.max(u,axis=0,keepdims=True)
            e=jnp.exp2(u-m)
            l=jnp.sum(e,axis=0,keepdims=True)
            w=jnp.sum(e*D,axis=0,keepdims=True)
            r=1.0/l
            dl=w*r
            Pm=e*r
            dS=(Pm*(D-dl)).astype(bf16)
            Pl=Pm.astype(bf16)
            w0=i*HD
            pt[:,w0:w0+pair*HD]=Pl
            dst[:,w0:w0+pair*HD]=dS
            if mode==0:
                dQT=lax.dot_general(KT,dS,NN,preferred_element_type=f32)
                for uu,c in enumerate(cols):
                    dq[:,c]=(dQT[:,uu*HD:(uu+1)*HD].T*SCALE).astype(bf16)
            elif mode==1:
                dQ=lax.dot_general(dS,K,TN,preferred_element_type=f32)*SCALE
                for uu,c in enumerate(cols):
                    dq[:,c]=dQ[uu*HD:(uu+1)*HD].astype(bf16)
        Qf=jnp.concatenate([q[:,i*HD:(i+1)*HD] for i in range(GRP)],axis=0)
        Gf=jnp.concatenate([g[:,i*HD:(i+1)*HD] for i in range(GRP)],axis=0)
        dK=lax.dot_general(dst[...],Qf,NN,preferred_element_type=f32)*SCALE
        dV=lax.dot_general(pt[...],Gf,NN,preferred_element_type=f32)
        acc[pl.ds(off,WIN),0:128]+=dK
        acc[pl.ds(off,WIN),128:256]+=dV
    dy[...]=acc[0:256].astype(bf16); dx[...]=acc[256:512].astype(bf16); do[...]=acc[512:768]

def chunk(scal, first, q, g, qr, gr, Y, X, O, c0, nk, prev=None, pair=4, mode=0):
    wide=GRP*HD
    own=lambda j,s:(0,s[0]+c0+j)
    oth=lambda j,s:(0,j)
    kvm=lambda j,s:(0,j)
    in_specs=[pl.BlockSpec((2,BLK),lambda j,s:(0,0)),
      pl.BlockSpec((BLK,wide),own),pl.BlockSpec((BLK,wide),own),
      pl.BlockSpec((BLK,wide),own),pl.BlockSpec((BLK,wide),own)]+[pl.BlockSpec((256,256),kvm)]*3
    args=[scal,first,q,qr,g,gr,Y,X,O]
    alias={}
    if prev is not None:
        in_specs+=[pl.BlockSpec(memory_space=pl.ANY)]
        alias={len(args):0}
        args+=[prev]
    out_shape=[jax.ShapeDtypeStruct(q.shape,bf16),jax.ShapeDtypeStruct((BLK,wide*nk),bf16)]+[jax.ShapeDtypeStruct((256,256*nk),bf16)]*2+[jax.ShapeDtypeStruct((256,256*nk),f32)]
    out_specs=[pl.BlockSpec((BLK,wide),own),pl.BlockSpec((BLK,wide),oth)]+[pl.BlockSpec((256,256),kvm)]*3
    return pl.pallas_call(functools.partial(kernel,pair=pair,mode=mode),
      grid_spec=pltpu.PrefetchScalarGridSpec(num_scalar_prefetch=1,grid=(nk,),in_specs=in_specs,out_specs=out_specs,
        scratch_shapes=[pltpu.VMEM((768,256),bf16),pltpu.VMEM((2,WIN,BLK),f32),pltpu.VMEM((WIN,GRP*HD),bf16),pltpu.VMEM((WIN,GRP*HD),bf16),pltpu.VMEM((768,256),f32)]),
      out_shape=out_shape,input_output_aliases=alias,
      compiler_params=pltpu.CompilerParams(vmem_limit_bytes=48*1024*1024,dimension_semantics=("arbitrary",)),
      cost_estimate=pl.CostEstimate(flops=4*nk*2*5*2*1024*640*128,bytes_accessed=nk*2*2**20,transcendentals=0),
      name="band_grads")(*args)


CHUNKS = (2,2)
AXES = ("ctx", "head")
ANY = pl.BlockSpec(memory_space=pl.ANY)


def rolled(value, steps):
    count = lax.axis_size("ctx") * lax.axis_size("head")
    return lax.ppermute(value, AXES, [(s, (s + steps) % count) for s in range(count)])


def core_swapped(value):
    count = lax.axis_size("ctx") * lax.axis_size("head")
    return lax.ppermute(value, AXES, [(s, s ^ 1) for s in range(count)])


def small_call(body, scal, args, in_specs, out_specs, out_shape, alias, name, moved):
    return pl.pallas_call(
        body,
        grid_spec=pltpu.PrefetchScalarGridSpec(
            num_scalar_prefetch=1, grid=(1,), in_specs=in_specs, out_specs=out_specs
        ),
        out_shape=out_shape,
        input_output_aliases=alias,
        compiler_params=pltpu.CompilerParams(vmem_limit_bytes=32 * 1024 * 1024),
        cost_estimate=pl.CostEstimate(flops=0, bytes_accessed=moved, transcendentals=0),
        name=name,
    )(scal, *args)


def assemble(scal, key_vectors, value_vectors, key_other, value_other):
    rows, width = key_vectors.shape
    half = width // 2

    def body(s, km, vm, kt, vt, *outs):
        here = pl.multiple_of(s[1] * rows, rows)
        there = pl.multiple_of((1 - s[1]) * rows, rows)
        c = 0
        for nk, out in zip(CHUNKS, outs):
            for i in range(nk):
                for k, v, at in ((km, vm, here), (kt, vt, there)):
                    out[pl.ds(at, rows), 2 * i * HD : (2 * i + 1) * HD] = k[:, c : c + HD]
                    out[pl.ds(at, rows), (2 * i + 1) * HD : (2 * i + 2) * HD] = v[:, c : c + HD]
                c += HD

    own = pl.BlockSpec((rows, half), lambda j, s: (0, s[1]))
    sizes = [2 * HD * nk for nk in CHUNKS]
    return small_call(
        body, scal, (key_vectors, value_vectors, key_other, value_other), [own] * 4,
        [pl.BlockSpec((2 * rows, size), lambda j, s: (0, 0)) for size in sizes],
        [jax.ShapeDtypeStruct((2 * rows, size), bf16) for size in sizes],
        {}, "assemble", 4 * rows * width * 2,
    )


def add_parts(scal, do, rx, ry, c0, prev):
    size = do.shape[1]
    half = 8 * HD // 2

    def body(s, o, x, y, *rest):
        gk, gv, sent = rest[-3:]
        here = pl.multiple_of(s[1] * BLK, BLK)
        there = pl.multiple_of((1 - s[1]) * BLK, BLK)

        def rows(at):
            return (
                o[pl.ds(at, BLK), :] + x[pl.ds(at, BLK), :].astype(f32) + y[pl.ds(at, BLK), :].astype(f32)
            ).astype(bf16)

        sent[...] = rows(there)
        stay = rows(here)
        for c in range(0, size, 2 * HD):
            gk[:, c // 2 : c // 2 + HD] = stay[:, c : c + HD]
            gv[:, c // 2 : c // 2 + HD] = stay[:, c + HD : c + 2 * HD]

    whole = pl.BlockSpec((2 * BLK, size), lambda j, s: (0, 0))
    per = half * 2 // size
    at = c0 * 2 * HD // size
    out_specs = [pl.BlockSpec((BLK, size // 2), lambda j, s: (0, s[1] * per + at))] * 2
    out_specs += [pl.BlockSpec((BLK, size), lambda j, s: (0, at))]
    shape = jax.ShapeDtypeStruct((BLK, 8 * HD), bf16)
    args, in_specs, alias = (do, rx, ry), [whole] * 3, {}
    if prev is not None:
        args, in_specs, alias = args + tuple(prev), in_specs + [ANY] * 3, {4: 0, 5: 1, 6: 2}
    return small_call(
        body, scal, args, in_specs, out_specs, [shape] * 3, alias, "add_parts", 512 * size * 8
    )


def place_key_grads(scal, gk, gv, back):
    rows, width = back.shape
    half = width // 2

    def body(s, b, k_in, v_in, k_out, v_out):
        for c in range(0, half, HD):
            k_out[:, c : c + HD] = b[:, 2 * c : 2 * c + HD]
            v_out[:, c : c + HD] = b[:, 2 * c + HD : 2 * c + 2 * HD]

    other = pl.BlockSpec((rows, half), lambda j, s: (0, 1 - s[1]))
    shape = jax.ShapeDtypeStruct((rows, width), bf16)
    return small_call(
        body, scal, (back, gk, gv), [pl.BlockSpec((rows, width), lambda j, s: (0, 0)), ANY, ANY],
        [other, other], [shape, shape], {2: 0, 3: 1}, "place_key_grads", 4 * rows * width,
    )


def place_query_grads(scal, dq, backs):
    rows, half = dq.shape[0], dq.shape[1] // 2

    def body(s, *refs):
        out = refs[-1]
        c = 0
        for b in refs[:-2]:
            out[:, c : c + b.shape[1]] = b[...]
            c += b.shape[1]

    return small_call(
        body, scal, (*backs, dq),
        [pl.BlockSpec(b.shape, lambda j, s: (0, 0)) for b in backs] + [ANY],
        pl.BlockSpec((rows, half), lambda j, s: (0, 1 - s[1])),
        jax.ShapeDtypeStruct(dq.shape, bf16), {len(backs) + 1: 0}, "place_query_grads", 4 * rows * half,
    )


def per_device(queries, key_vectors, value_vectors, out_grad, doc_starts):
    head = lax.axis_index("head")
    core = head % 2
    chip = lax.axis_index("ctx") * 2 + head // 2
    scal = jnp.stack([core * 4, core]).astype(jnp.int32)
    own = assemble(
        scal, key_vectors, value_vectors, core_swapped(key_vectors), core_swapped(value_vectors)
    )
    queries, out_grad, own = lax.optimization_barrier((queries, out_grad, tuple(own)))
    query_other = core_swapped(queries)
    grad_other = core_swapped(out_grad)
    rows = jnp.stack([core, 1 - core])[:, None] * BLK + jnp.arange(BLK)[None, :] + chip * 256
    reached = jnp.where(doc_starts[None, None, :] <= rows[:, :, None], doc_starts[None, None, :], 0)
    first = jnp.max(reached, axis=-1) - (chip * 256 - 512)
    offsets = [sum(CHUNKS[:i]) for i in range(len(CHUNKS))]
    moved = []
    for i, part in enumerate(own):
        if i >= 2:
            moved[i - 2], query_other, grad_other, part = lax.optimization_barrier(
                (moved[i - 2], query_other, grad_other, part)
            )
        moved.append((rolled(part, 4), rolled(part, 2), part))
    dqa = None
    parts = []
    backs = []
    for c0, nk, (y, x, o) in zip(offsets, CHUNKS, moved):
        dqa, dqb, dy, dx, do = chunk(
            scal, first, queries, out_grad, query_other, grad_other, y, x, o, c0, nk, dqa
        )
        if parts:
            parts[-1], dx, dy = lax.optimization_barrier((parts[-1], dx, dy))
        parts.append((do, rolled(dx, -2), rolled(dy, -4)))
        backs.append(core_swapped(dqb))
    grad_query = place_query_grads(scal, dqa, backs)
    sums = None
    for c0, part in zip(offsets, parts):
        sums = add_parts(scal, *part, c0, sums)
    grad_key, grad_value = place_key_grads(scal, sums[0], sums[1], core_swapped(sums[2]))
    return (grad_query, grad_key, grad_value)


def solution(mesh):
    split = P(AXES, None)
    return jax.shard_map(
        per_device,
        mesh=mesh,
        in_specs=(split, split, split, split, P()),
        out_specs=(split, split, split),
        check_vma=False,
    )
```

profile of v0, /device:TPU:1, one launch (start us, length us, event | category | flops | bytes accessed | tf_op | source)
XLA Modules:
  0.0 84.7 jit_solution(10708757545444045298)
XLA Ops:
  0.6 3.3 %collective-permute-start = (bf16[128,1024]{1,0:T(8,128)(2,1)}, bf16[128,1024]{1,0:T(8,128)(2,1)S(1)}, u32[]{:S(2)}, u32[]{:S(2)}) collective-permute-start(bf16[128,1024]{1,0:T(8,128)(2,1)} %km.1), channel_id=1, source_target_pairs={{0,1},{1,0},{2,3},{3,2},{4,5},{5,4},{6,7},{7,6},{8,9},{9,8},{10,11... | collective-permute-start | bytes 786440 | tf_op jit(solution)/shard_map/ppermute | solution.py:105
  4.0 0.1 collective-permute-start.1
  4.1 0.1 pad_add_fusion.s.scal
  4.1 1.2 %collective-permute-done.kt = bf16[128,1024]{1,0:T(8,128)(2,1)S(1)} collective-permute-done((bf16[128,1024]{1,0:T(8,128)(2,1)}, bf16[128,1024]{1,0:T(8,128)(2,1)S(1)}, u32[]{:S(2)}, u32[]{:S(2)}) %collective-permute-start) | collective-permute-done | bytes 262176 | tf_op jit(solution)/shard_map/ppermute | solution.py:105
  5.3 0.4 collective-permute-done.1.vt
  5.7 0.0 copy-start
  5.7 0.9 %copy-done = bf16[128,1024]{1,0:T(8,128)(2,1)S(1)} copy-done((bf16[128,1024]{1,0:T(8,128)(2,1)S(1)}, bf16[128,1024]{1,0:T(8,128)(2,1)}, u32[]{:S(2)}) %copy-start) | copy-done | bytes 262168
  6.7 0.0 copy-start.1
  6.7 0.9 %copy-done.1 = bf16[128,1024]{1,0:T(8,128)(2,1)S(1)} copy-done((bf16[128,1024]{1,0:T(8,128)(2,1)S(1)}, bf16[128,1024]{1,0:T(8,128)(2,1)}, u32[]{:S(2)}) %copy-start.1) | copy-done | bytes 262168
  7.6 0.7 assemble.1
  8.3 0.5 collective-permute-start.2
  8.7 0.1 collective-permute-start.3
  8.9 0.1 add_multiply_fusion
  9.0 0.1 add_add_fusion
  9.0 0.0 collective-permute-start.5
  9.0 0.8 collective-permute-start.4
  9.8 0.9 %fusion = s32[2,128]{1,0:T(2,128)S(1)} fusion(s32[2,128]{1,0:T(2,128)S(1)} %add_add_fusion, s32[127]{0:T(128)} %param.9), kind=kLoop, calls=%fused_computation.1 | loop fusion | flops 97280 | bytes 2556 | tf_op jit(solution)/shard_map/reduce_max | solution.py:229
  10.7 1.3 %collective-permute-start.8 = (bf16[256,512]{1,0:T(8,128)(2,1)S(1)}, bf16[256,512]{1,0:T(8,128)(2,1)S(1)}, u32[]{:S(2)}, u32[]{:S(2)}) collective-permute-start(bf16[256,512]{1,0:T(8,128)(2,1)S(1)} %get-tuple-element.38.o_ref), channel_id=1, source_target_pairs={{0,2},{1,3},{2,4},{3,5},{4,6},{5,7},{6,8},{7,9},{8,10},{9,11},{10,... | collective-permute-start | bytes 786440 | tf_op jit(solution)/shard_map/ppermute | solution.py:100
  12.0 15.2 %collective-permute-done.5.x_ref = bf16[256,512]{1,0:T(8,128)(2,1)S(1)} collective-permute-done((bf16[256,512]{1,0:T(8,128)(2,1)S(1)}, bf16[256,512]{1,0:T(8,128)(2,1)S(1)}, u32[]{:S(2)}, u32[]{:S(2)}) %collective-permute-start.5) | collective-permute-done | bytes 262176 | tf_op jit(solution)/shard_map/ppermute | solution.py:100
  27.3 0.0 collective-permute-start.7
  27.3 1.6 %collective-permute-done.4.y_ref = bf16[256,512]{1,0:T(8,128)(2,1)S(1)} collective-permute-done((bf16[256,512]{1,0:T(8,128)(2,1)S(1)}, bf16[256,512]{1,0:T(8,128)(2,1)S(1)}, u32[]{:S(2)}, u32[]{:S(2)}) %collective-permute-start.4) | collective-permute-done | bytes 262176 | tf_op jit(solution)/shard_map/ppermute | solution.py:100
  28.9 0.0 collective-permute-done.2.qb
  28.9 0.0 copy-start.3
  28.9 0.0 collective-permute-done.3.gb
  28.9 1.3 %copy-done.3 = bf16[128,8192]{1,0:T(8,128)(2,1)} copy-done((bf16[128,8192]{1,0:T(8,128)(2,1)}, bf16[128,8192]{1,0:T(8,128)(2,1)S(1)}, u32[]{:S(2)}) %copy-start.3) | copy-done | bytes 2097176
  30.2 0.0 copy-start.2
  30.2 1.6 %copy-done.2 = bf16[128,8192]{1,0:T(8,128)(2,1)S(1)} copy-done((bf16[128,8192]{1,0:T(8,128)(2,1)S(1)}, bf16[128,8192]{1,0:T(8,128)(2,1)}, u32[]{:S(2)}) %copy-start.2) | copy-done | bytes 2097176
  31.8 12.8 %band_grads.2 = (bf16[128,8192]{1,0:T(8,128)(2,1)}, bf16[128,2048]{1,0:T(8,128)(2,1)S(1)}, bf16[256,512]{1,0:T(8,128)(2,1)S(1)}, bf16[256,512]{1,0:T(8,128)(2,1)S(1)}, f32[256,512]{1,0:T(8,128)S(1)}) custom-call(s32[2]{0:T(128)S(1)} %pad_add_fusion.s.scal, s32[2,128]{1,0:T(2,128)S(1)} %broadcast_subtract_fusion.first_ref, bf16[128,8192]{1,0:T(8,128)(2,1)S(1)} %copy-done.2, ...), custom_call_target="tpu_custom_call" | custom-call | flops 13421772800 | bytes 4194304 | tf_op jit(solution)/shard_map/band_grads/pallas_call | solution.py:84
  44.6 1.5 %collective-permute-start.10 = (bf16[256,512]{1,0:T(8,128)(2,1)S(1)}, bf16[256,512]{1,0:T(8,128)(2,1)S(1)}, u32[]{:S(2)}, u32[]{:S(2)}) collective-permute-start(bf16[256,512]{1,0:T(8,128)(2,1)S(1)} %get-tuple-element.44), channel_id=1, source_target_pairs={{0,254},{1,255},{2,0},{3,1},{4,2},{5,3},{6,4},{7,5},{8,6},{9,7},{1... | collective-permute-start | bytes 786440 | tf_op jit(solution)/shard_map/ppermute | solution.py:100
  46.1 7.9 %collective-permute-start.11 = (bf16[256,512]{1,0:T(8,128)(2,1)S(1)}, bf16[256,512]{1,0:T(8,128)(2,1)S(1)}, u32[]{:S(2)}, u32[]{:S(2)}) collective-permute-start(bf16[256,512]{1,0:T(8,128)(2,1)S(1)} %get-tuple-element.45), channel_id=1, source_target_pairs={{0,252},{1,253},{2,254},{3,255},{4,0},{5,1},{6,2},{7,3},{8,4},{9,5... | collective-permute-start | bytes 786440 | tf_op jit(solution)/shard_map/ppermute | solution.py:100
  54.0 0.0 collective-permute-done.8.x_ref
  54.0 0.0 collective-permute-done.7.y_ref
  54.0 12.8 %band_grads.3 = (bf16[128,8192]{1,0:T(8,128)(2,1)}, bf16[128,2048]{1,0:T(8,128)(2,1)S(1)}, bf16[256,512]{1,0:T(8,128)(2,1)S(1)}, bf16[256,512]{1,0:T(8,128)(2,1)S(1)}, f32[256,512]{1,0:T(8,128)S(1)}) custom-call(s32[2]{0:T(128)S(1)} %pad_add_fusion.s.scal, s32[2,128]{1,0:T(2,128)S(1)} %broadcast_subtract_fusion.first_ref, ...), custom_call_target="tpu_custom_call", output_to_operand_aliasing={{0}: (9, {})} | custom-call | flops 13421772800 | bytes 4194304 | tf_op jit(solution)/shard_map/band_grads/pallas_call | solution.py:84
  66.8 0.0 collective-permute-done.10.x
  66.8 0.0 collective-permute-done.11.y
  66.8 0.6 collective-permute-start.12
  67.4 1.1 %collective-permute-start.13 = (bf16[256,512]{1,0:T(8,128)(2,1)S(1)}, bf16[256,512]{1,0:T(8,128)(2,1)S(1)}, u32[]{:S(2)}, u32[]{:S(2)}) collective-permute-start(bf16[256,512]{1,0:T(8,128)(2,1)S(1)} %get-tuple-element.49), channel_id=1, source_target_pairs={{0,252},{1,253},{2,254},{3,255},{4,0},{5,1},{6,2},{7,3},{8,4},{9,5... | collective-permute-start | bytes 786440 | tf_op jit(solution)/shard_map/ppermute | solution.py:100
  68.6 1.6 %collective-permute-start.9 = (bf16[128,2048]{1,0:T(8,128)(2,1)S(1)}, bf16[128,2048]{1,0:T(8,128)(2,1)S(1)}, u32[]{:S(2)}, u32[]{:S(2)}) collective-permute-start(bf16[128,2048]{1,0:T(8,128)(2,1)S(1)} %get-tuple-element.40), channel_id=1, source_target_pairs={{0,1},{1,0},{2,3},{3,2},{4,5},{5,4},{6,7},{7,6},{8,9},{9,8},{10,11... | collective-permute-start | bytes 1572872 | tf_op jit(solution)/shard_map/ppermute | solution.py:105
  70.2 0.0 collective-permute-start.6
  70.2 1.2 %add_parts.2 = (bf16[128,1024]{1,0:T(8,128)(2,1)}, bf16[128,1024]{1,0:T(8,128)(2,1)}, bf16[128,1024]{1,0:T(8,128)(2,1)S(1)}) custom-call(s32[2]{0:T(128)S(1)} %pad_add_fusion.s.scal, f32[256,512]{1,0:T(8,128)S(1)} %get-tuple-element.50.o, bf16[256,512]{1,0:T(8,128)(2,1)S(1)} %collective-permute-done.10.x, bf16[256,512]{1,0:T(8,128)(2,1)S(1)} %collective-permute-done.11.y), custom_call_target="tpu_custom_call" | custom-call | bytes 2097152 | tf_op jit(solution)/shard_map/add_parts/pallas_call | solution.py:109
  71.5 5.9 %collective-permute-done.12.x = bf16[256,512]{1,0:T(8,128)(2,1)S(1)} collective-permute-done((bf16[256,512]{1,0:T(8,128)(2,1)S(1)}, bf16[256,512]{1,0:T(8,128)(2,1)S(1)}, u32[]{:S(2)}, u32[]{:S(2)}) %collective-permute-start.12) | collective-permute-done | bytes 262176 | tf_op jit(solution)/shard_map/ppermute | solution.py:100
  77.4 1.1 %collective-permute-done.13.y = bf16[256,512]{1,0:T(8,128)(2,1)S(1)} collective-permute-done((bf16[256,512]{1,0:T(8,128)(2,1)S(1)}, bf16[256,512]{1,0:T(8,128)(2,1)S(1)}, u32[]{:S(2)}, u32[]{:S(2)}) %collective-permute-start.13) | collective-permute-done | bytes 262176 | tf_op jit(solution)/shard_map/ppermute | solution.py:100
  78.5 1.2 %add_parts.3 = (bf16[128,1024]{1,0:T(8,128)(2,1)}, bf16[128,1024]{1,0:T(8,128)(2,1)}, bf16[128,1024]{1,0:T(8,128)(2,1)S(1)}) custom-call(s32[2]{0:T(128)S(1)} %pad_add_fusion.s.scal, f32[256,512]{1,0:T(8,128)S(1)} %get-tuple-element.42.o, bf16[256,512]{1,0:T(8,128)(2,1)S(1)} %collective-permute-done.12.x, ...), custom_call_target="tpu_custom_call", output_to_operand_aliasing={{0}: (4, {}), {1}: (5, {}), {2}: (6, {})} | custom-call | bytes 2097152 | tf_op jit(solution)/shard_map/add_parts/pallas_call | solution.py:109
  79.8 2.1 %collective-permute-start.14 = (bf16[128,1024]{1,0:T(8,128)(2,1)S(1)}, bf16[128,1024]{1,0:T(8,128)(2,1)S(1)}, u32[]{:S(2)}, u32[]{:S(2)}) collective-permute-start(bf16[128,1024]{1,0:T(8,128)(2,1)S(1)} %get-tuple-element.56), channel_id=1, source_target_pairs={{0,1},{1,0},{2,3},{3,2},{4,5},{5,4},{6,7},{7,6},{8,9},{9,8},{10,11... | collective-permute-start | bytes 786440 | tf_op jit(solution)/shard_map/ppermute | solution.py:105
  81.8 0.0 collective-permute-done.9.refs_1_
  81.9 0.0 collective-permute-done.6.refs_0_
  81.9 1.6 %place_query_grads.1 = bf16[128,8192]{1,0:T(8,128)(2,1)} custom-call(s32[2]{0:T(128)S(1)} %pad_add_fusion.s.scal, bf16[128,2048]{1,0:T(8,128)(2,1)S(1)} %collective-permute-done.6.refs_0_, bf16[128,2048]{1,0:T(8,128)(2,1)S(1)} %collective-permute-done.9.refs_1_, bf16[128,8192]{1,0:T(8,128)(2,1)} %get-tuple-element.41.refs_2_), custom_call_target="tpu_custom_call", output_to_operand_aliasing={{}: (3, {})} | custom-call | bytes 2097152 | tf_op jit(solution)/shard_map/place_query_grads/pallas_call | solution.py:109
  83.4 0.0 collective-permute-done.14.b
  83.4 1.3 %place_key_grads.1 = (bf16[128,1024]{1,0:T(8,128)(2,1)}, bf16[128,1024]{1,0:T(8,128)(2,1)}) custom-call(s32[2]{0:T(128)S(1)} %pad_add_fusion.s.scal, bf16[128,1024]{1,0:T(8,128)(2,1)S(1)} %collective-permute-done.14.b, bf16[128,1024]{1,0:T(8,128)(2,1)} %get-tuple-element.57.k_in, ...), custom_call_target="tpu_custom_call", output_to_operand_aliasing={{0}: (2, {}), {1}: (3, {})} | custom-call | bytes 524288 | tf_op jit(solution)/shard_map/place_key_grads/pallas_call | solution.py:109
  (1 shorter events, 0.0 us)
Async XLA Ops:
  0.6 4.7 %collective-permute-start = (bf16[128,1024]{1,0:T(8,128)(2,1)}, bf16[128,1024]{1,0:T(8,128)(2,1)S(1)}, u32[]{:S(2)}, u32[]{:S(2)}) collective-permute-start(bf16[128,1024]{1,0:T(8,128)(2,1)} %km.1), channel_id=1, source_target_pairs={{0,1},{1,0},{2,3},{3,2},{4,5},{5,4},{6,7},{7,6},{8,9},{9,8},{10,11... | collective-permute-start | bytes 786440 | tf_op jit(solution)/shard_map/ppermute | solution.py:105
  4.0 1.7 %collective-permute-start.1 = (bf16[128,1024]{1,0:T(8,128)(2,1)}, bf16[128,1024]{1,0:T(8,128)(2,1)S(1)}, u32[]{:S(2)}, u32[]{:S(2)}) collective-permute-start(bf16[128,1024]{1,0:T(8,128)(2,1)} %vm.1), channel_id=1, source_target_pairs={{0,1},{1,0},{2,3},{3,2},{4,5},{5,4},{6,7},{7,6},{8,9},{9,8},{10,11... | collective-permute-start | bytes 786440 | tf_op jit(solution)/shard_map/ppermute | solution.py:105
  5.7 0.9 %copy-start = (bf16[128,1024]{1,0:T(8,128)(2,1)S(1)}, bf16[128,1024]{1,0:T(8,128)(2,1)}, u32[]{:S(2)}) copy-start(bf16[128,1024]{1,0:T(8,128)(2,1)} %km.1) | copy-start | bytes 786436
  6.7 0.9 %copy-start.1 = (bf16[128,1024]{1,0:T(8,128)(2,1)S(1)}, bf16[128,1024]{1,0:T(8,128)(2,1)}, u32[]{:S(2)}) copy-start(bf16[128,1024]{1,0:T(8,128)(2,1)} %vm.1) | copy-start | bytes 786436
  8.3 20.6 %collective-permute-start.2 = (bf16[128,8192]{1,0:T(8,128)(2,1)}, bf16[128,8192]{1,0:T(8,128)(2,1)S(1)}, u32[]{:S(2)}, u32[]{:S(2)}) collective-permute-start(bf16[128,8192]{1,0:T(8,128)(2,1)} %qa.1), channel_id=1, source_target_pairs={{0,1},{1,0},{2,3},{3,2},{4,5},{5,4},{6,7},{7,6},{8,9},{9,8},{10,11... | collective-permute-start | bytes 6291464 | tf_op jit(solution)/shard_map/ppermute | solution.py:105
  8.7 20.2 %collective-permute-start.3 = (bf16[128,8192]{1,0:T(8,128)(2,1)}, bf16[128,8192]{1,0:T(8,128)(2,1)}, u32[]{:S(2)}, u32[]{:S(2)}) collective-permute-start(bf16[128,8192]{1,0:T(8,128)(2,1)} %ga.1), channel_id=1, source_target_pairs={{0,1},{1,0},{2,3},{3,2},{4,5},{5,4},{6,7},{7,6},{8,9},{9,8},{10,11... | collective-permute-start | bytes 6291464 | tf_op jit(solution)/shard_map/ppermute | solution.py:105
  9.0 18.2 %collective-permute-start.5 = (bf16[256,512]{1,0:T(8,128)(2,1)S(1)}, bf16[256,512]{1,0:T(8,128)(2,1)S(1)}, u32[]{:S(2)}, u32[]{:S(2)}) collective-permute-start(bf16[256,512]{1,0:T(8,128)(2,1)S(1)} %get-tuple-element.36.o_ref), channel_id=1, source_target_pairs={{0,2},{1,3},{2,4},{3,5},{4,6},{5,7},{6,8},{7,9},{8,10},{9,11},{10,... | collective-permute-start | bytes 786440 | tf_op jit(solution)/shard_map/ppermute | solution.py:100
  9.0 19.9 %collective-permute-start.4 = (bf16[256,512]{1,0:T(8,128)(2,1)S(1)}, bf16[256,512]{1,0:T(8,128)(2,1)S(1)}, u32[]{:S(2)}, u32[]{:S(2)}) collective-permute-start(bf16[256,512]{1,0:T(8,128)(2,1)S(1)} %get-tuple-element.36.o_ref), channel_id=1, source_target_pairs={{0,4},{1,5},{2,6},{3,7},{4,8},{5,9},{6,10},{7,11},{8,12},{9,13},{1... | collective-permute-start | bytes 786440 | tf_op jit(solution)/shard_map/ppermute | solution.py:100
  10.7 43.4 %collective-permute-start.8 = (bf16[256,512]{1,0:T(8,128)(2,1)S(1)}, bf16[256,512]{1,0:T(8,128)(2,1)S(1)}, u32[]{:S(2)}, u32[]{:S(2)}) collective-permute-start(bf16[256,512]{1,0:T(8,128)(2,1)S(1)} %get-tuple-element.38.o_ref), channel_id=1, source_target_pairs={{0,2},{1,3},{2,4},{3,5},{4,6},{5,7},{6,8},{7,9},{8,10},{9,11},{10,... | collective-permute-start | bytes 786440 | tf_op jit(solution)/shard_map/ppermute | solution.py:100
  27.3 26.8 %collective-permute-start.7 = (bf16[256,512]{1,0:T(8,128)(2,1)S(1)}, bf16[256,512]{1,0:T(8,128)(2,1)S(1)}, u32[]{:S(2)}, u32[]{:S(2)}) collective-permute-start(bf16[256,512]{1,0:T(8,128)(2,1)S(1)} %get-tuple-element.38.o_ref), channel_id=1, source_target_pairs={{0,4},{1,5},{2,6},{3,7},{4,8},{5,9},{6,10},{7,11},{8,12},{9,13},{1... | collective-permute-start | bytes 786440 | tf_op jit(solution)/shard_map/ppermute | solution.py:100
  28.9 1.3 %copy-start.3 = (bf16[128,8192]{1,0:T(8,128)(2,1)}, bf16[128,8192]{1,0:T(8,128)(2,1)S(1)}, u32[]{:S(2)}) copy-start(bf16[128,8192]{1,0:T(8,128)(2,1)S(1)} %collective-permute-done.2.qb) | copy-start | bytes 6291460
  30.2 1.6 %copy-start.2 = (bf16[128,8192]{1,0:T(8,128)(2,1)S(1)}, bf16[128,8192]{1,0:T(8,128)(2,1)}, u32[]{:S(2)}) copy-start(bf16[128,8192]{1,0:T(8,128)(2,1)} %qa.1) | copy-start | bytes 6291460
  44.6 22.2 %collective-permute-start.10 = (bf16[256,512]{1,0:T(8,128)(2,1)S(1)}, bf16[256,512]{1,0:T(8,128)(2,1)S(1)}, u32[]{:S(2)}, u32[]{:S(2)}) collective-permute-start(bf16[256,512]{1,0:T(8,128)(2,1)S(1)} %get-tuple-element.44), channel_id=1, source_target_pairs={{0,254},{1,255},{2,0},{3,1},{4,2},{5,3},{6,4},{7,5},{8,6},{9,7},{1... | collective-permute-start | bytes 786440 | tf_op jit(solution)/shard_map/ppermute | solution.py:100
  46.1 20.7 %collective-permute-start.11 = (bf16[256,512]{1,0:T(8,128)(2,1)S(1)}, bf16[256,512]{1,0:T(8,128)(2,1)S(1)}, u32[]{:S(2)}, u32[]{:S(2)}) collective-permute-start(bf16[256,512]{1,0:T(8,128)(2,1)S(1)} %get-tuple-element.45), channel_id=1, source_target_pairs={{0,252},{1,253},{2,254},{3,255},{4,0},{5,1},{6,2},{7,3},{8,4},{9,5... | collective-permute-start | bytes 786440 | tf_op jit(solution)/shard_map/ppermute | solution.py:100
  66.8 10.6 %collective-permute-start.12 = (bf16[256,512]{1,0:T(8,128)(2,1)S(1)}, bf16[256,512]{1,0:T(8,128)(2,1)S(1)}, u32[]{:S(2)}, u32[]{:S(2)}) collective-permute-start(bf16[256,512]{1,0:T(8,128)(2,1)S(1)} %get-tuple-element.48), channel_id=1, source_target_pairs={{0,254},{1,255},{2,0},{3,1},{4,2},{5,3},{6,4},{7,5},{8,6},{9,7},{1... | collective-permute-start | bytes 786440 | tf_op jit(solution)/shard_map/ppermute | solution.py:100
  67.4 11.1 %collective-permute-start.13 = (bf16[256,512]{1,0:T(8,128)(2,1)S(1)}, bf16[256,512]{1,0:T(8,128)(2,1)S(1)}, u32[]{:S(2)}, u32[]{:S(2)}) collective-permute-start(bf16[256,512]{1,0:T(8,128)(2,1)S(1)} %get-tuple-element.49), channel_id=1, source_target_pairs={{0,252},{1,253},{2,254},{3,255},{4,0},{5,1},{6,2},{7,3},{8,4},{9,5... | collective-permute-start | bytes 786440 | tf_op jit(solution)/shard_map/ppermute | solution.py:100
  68.6 13.3 %collective-permute-start.9 = (bf16[128,2048]{1,0:T(8,128)(2,1)S(1)}, bf16[128,2048]{1,0:T(8,128)(2,1)S(1)}, u32[]{:S(2)}, u32[]{:S(2)}) collective-permute-start(bf16[128,2048]{1,0:T(8,128)(2,1)S(1)} %get-tuple-element.40), channel_id=1, source_target_pairs={{0,1},{1,0},{2,3},{3,2},{4,5},{5,4},{6,7},{7,6},{8,9},{9,8},{10,11... | collective-permute-start | bytes 1572872 | tf_op jit(solution)/shard_map/ppermute | solution.py:105
  70.2 11.6 %collective-permute-start.6 = (bf16[128,2048]{1,0:T(8,128)(2,1)S(1)}, bf16[128,2048]{1,0:T(8,128)(2,1)S(1)}, u32[]{:S(2)}, u32[]{:S(2)}) collective-permute-start(bf16[128,2048]{1,0:T(8,128)(2,1)S(1)} %get-tuple-element.37), channel_id=1, source_target_pairs={{0,1},{1,0},{2,3},{3,2},{4,5},{5,4},{6,7},{7,6},{8,9},{9,8},{10,11... | collective-permute-start | bytes 1572872 | tf_op jit(solution)/shard_map/ppermute | solution.py:105
  79.8 3.7 %collective-permute-start.14 = (bf16[128,1024]{1,0:T(8,128)(2,1)S(1)}, bf16[128,1024]{1,0:T(8,128)(2,1)S(1)}, u32[]{:S(2)}, u32[]{:S(2)}) collective-permute-start(bf16[128,1024]{1,0:T(8,128)(2,1)S(1)} %get-tuple-element.56), channel_id=1, source_target_pairs={{0,1},{1,0},{2,3},{3,2},{4,5},{5,4},{6,7},{7,6},{8,9},{9,8},{10,11... | collective-permute-start | bytes 786440 | tf_op jit(solution)/shard_map/ppermute | solution.py:105
where the time goes:
time: 85 us; the launch traced here: 84.7 us
  Pallas kernels  31.5 us (37%)
  waiting for transfers between devices  25.5 us (30%)
  starting transfers between devices  21.1 us (25%)
  local copies, waits for them, and re-layouts  4.81 us (6%)
  other arithmetic  1.09 us (1%)
    pallas_call x2, Pallas kernels, chunk(): pl.pallas_call(functools.partial(kernel, pair=pair, mode=mode), grid_spec...  25.5 us
    ppermute x8, waiting for transfers between devices, rolled(): lax.ppermute(value, AXES, [(s, (s + steps) % count) for s in range(count)])  24 us
    ppermute x8, starting transfers between devices, rolled(): lax.ppermute(value, AXES, [(s, (s + steps) % count) for s in range(count)])  13.3 us
    ppermute x7, starting transfers between devices, core_swapped(): return lax.ppermute(value, AXES, [(s, s ^ 1) for s in range(count)])  7.73 us
    pallas_call x5, Pallas kernels, small_call(): pl.pallas_call(body, grid_spec=pltpu.PrefetchScalarGridSpec(num_scalar_pr...  6.01 us
    unnamed x8, local copies, waits for them, and re-layouts  4.81 us
  transfers between devices with their start and end apart: 15, of which 6 were waited for; matrix products, arithmetic and copies ran while one was open for 1% of the time, Pallas kernels for 35%

commit v1 on v0

--- a/solution.py
+++ b/solution.py
@@ -10,6 +10,39 @@
 NN=(((1,),(0,)),((),()))
 TN=(((0,),(0,)),((),()))
 f32=jnp.float32; bf16=jnp.bfloat16
+
+def one_set(q,g,dq,off,win,bias,kv,pt,dst,acc,pair):
+    K=kv[pl.ds(off,win),0:128]; V=kv[pl.ds(off,win),128:256]; KT=K.T
+    b=jnp.concatenate([bias[...]]*pair,axis=1)
+    def rows(ref,i):
+        return jnp.concatenate([ref[:,(i+u)*HD:(i+u+1)*HD] for u in range(pair)],axis=0)
+    def scores(i):
+        S=lax.dot_general(K,rows(q,i),TT,preferred_element_type=f32)
+        D=lax.dot_general(V,rows(g,i),TT,preferred_element_type=f32)
+        return S,D
+    ahead=scores(0)
+    for i in range(0,GRP,pair):
+        S,D=ahead
+        if i+pair<GRP: ahead=scores(i+pair)
+        u=S*(SCALE*LOG2E)+b
+        m=jnp.max(u,axis=0,keepdims=True)
+        e=jnp.exp2(u-m)
+        l=jnp.sum(e,axis=0,keepdims=True)
+        w=jnp.sum(e*D,axis=0,keepdims=True)
+        r=1.0/l
+        dl=w*r
+        Pm=e*r
+        dS=(Pm*(D-dl)).astype(bf16)
+        pt[0:win,i*HD:(i+pair)*HD]=Pm.astype(bf16)
+        dst[0:win,i*HD:(i+pair)*HD]=dS
+        dQT=lax.dot_general(KT,dS,NN,preferred_element_type=f32)
+        for uu in range(pair):
+            dq[:,(i+uu)*HD:(i+uu+1)*HD]=(dQT[:,uu*HD:(uu+1)*HD].T*SCALE).astype(bf16)
+    acc[pl.ds(off,win),0:128]+=lax.dot_general(dst[0:win],rows_all(q),NN,preferred_element_type=f32)*SCALE
+    acc[pl.ds(off,win),128:256]+=lax.dot_general(pt[0:win],rows_all(g),NN,preferred_element_type=f32)
+
+def rows_all(ref):
+    return jnp.concatenate([ref[:,c*HD:(c+1)*HD] for c in range(GRP)],axis=0)
 
 def kernel(scal, first_ref, qa, qb, ga, gb, y_ref, x_ref, o_ref, *rest, pair, mode):
     dqa, dqb, dy, dx, do, kv, bias, pt, dst, acc = rest[-10:]
@@ -26,43 +59,10 @@
             bias[s]=jnp.where(ok,0.0,-1e30).astype(f32)
     acc[...]=jnp.zeros_like(acc)
     for s,(q,g,dq,off) in enumerate(((qa,ga,dqa,off_a),(qb,gb,dqb,off_b))):
-        K=kv[pl.ds(off,WIN),0:128]; V=kv[pl.ds(off,WIN),128:256]
-        KT=K.T
-        for i in range(0,GRP,pair):
-            cols=[slice((i+u)*HD,(i+u+1)*HD) for u in range(pair)]
-            Q=jnp.concatenate([q[:,c] for c in cols],axis=0)
-            G=jnp.concatenate([g[:,c] for c in cols],axis=0)
-            S=lax.dot_general(K,Q,TT,preferred_element_type=f32)
-            D=lax.dot_general(V,G,TT,preferred_element_type=f32)
-            b=bias[s]
-            b=jnp.concatenate([b]*pair,axis=1)
-            u=S*(SCALE*LOG2E)+b
-            m=jnp.max(u,axis=0,keepdims=True)
-            e=jnp.exp2(u-m)
-            l=jnp.sum(e,axis=0,keepdims=True)
-            w=jnp.sum(e*D,axis=0,keepdims=True)
-            r=1.0/l
-            dl=w*r
-            Pm=e*r
-            dS=(Pm*(D-dl)).astype(bf16)
-            Pl=Pm.astype(bf16)
-            w0=i*HD
-            pt[:,w0:w0+pair*HD]=Pl
-            dst[:,w0:w0+pair*HD]=dS
-            if mode==0:
-                dQT=lax.dot_general(KT,dS,NN,preferred_element_type=f32)
-                for uu,c in enumerate(cols):
-                    dq[:,c]=(dQT[:,uu*HD:(uu+1)*HD].T*SCALE).astype(bf16)
-            elif mode==1:
-                dQ=lax.dot_general(dS,K,TN,preferred_element_type=f32)*SCALE
-                for uu,c in enumerate(cols):
-                    dq[:,c]=dQ[uu*HD:(uu+1)*HD].astype(bf16)
-        Qf=jnp.concatenate([q[:,i*HD:(i+1)*HD] for i in range(GRP)],axis=0)
-        Gf=jnp.concatenate([g[:,i*HD:(i+1)*HD] for i in range(GRP)],axis=0)
-        dK=lax.dot_general(dst[...],Qf,NN,preferred_element_type=f32)*SCALE
-        dV=lax.dot_general(pt[...],Gf,NN,preferred_element_type=f32)
-        acc[pl.ds(off,WIN),0:128]+=dK
-        acc[pl.ds(off,WIN),128:256]+=dV
+        for skip in range(4):
+            @pl.when(scal[2+s]==skip)
+            def _(s=s,q=q,g=g,dq=dq,off=off,skip=skip):
+                one_set(q,g,dq,pl.multiple_of(off+skip*BLK,BLK),WIN-skip*BLK,bias.at[s,pl.ds(skip*BLK,WIN-skip*BLK)],kv,pt,dst,acc,pair)
     dy[...]=acc[0:256].astype(bf16); dx[...]=acc[256:512].astype(bf16); do[...]=acc[512:768]
 
 def chunk(scal, first, q, g, qr, gr, Y, X, O, c0, nk, prev=None, pair=4, mode=0):
@@ -90,7 +90,8 @@
       name="band_grads")(*args)
 
 
-CHUNKS = (2,2)
+CHUNKS = (2, 2)
+LIMIT = 32 * 1024 * 1024
 AXES = ("ctx", "head")
 ANY = pl.BlockSpec(memory_space=pl.ANY)
 
@@ -113,7 +114,7 @@
         ),
         out_shape=out_shape,
         input_output_aliases=alias,
-        compiler_params=pltpu.CompilerParams(vmem_limit_bytes=32 * 1024 * 1024),
+        compiler_params=pltpu.CompilerParams(vmem_limit_bytes=LIMIT),
         cost_estimate=pl.CostEstimate(flops=0, bytes_accessed=moved, transcendentals=0),
         name=name,
     )(scal, *args)
@@ -227,20 +228,18 @@
     rows = jnp.stack([core, 1 - core])[:, None] * BLK + jnp.arange(BLK)[None, :] + chip * 256
     reached = jnp.where(doc_starts[None, None, :] <= rows[:, :, None], doc_starts[None, None, :], 0)
     first = jnp.max(reached, axis=-1) - (chip * 256 - 512)
+    skips = jnp.clip((first[:, 0] - jnp.stack([core, 1 - core]) * BLK) // BLK, 0, 3)
+    band_scal = jnp.concatenate([scal, skips.astype(jnp.int32)])
     offsets = [sum(CHUNKS[:i]) for i in range(len(CHUNKS))]
     moved = []
     for i, part in enumerate(own):
-        if i >= 2:
-            moved[i - 2], query_other, grad_other, part = lax.optimization_barrier(
-                (moved[i - 2], query_other, grad_other, part)
-            )
         moved.append((rolled(part, 4), rolled(part, 2), part))
     dqa = None
     parts = []
     backs = []
     for c0, nk, (y, x, o) in zip(offsets, CHUNKS, moved):
         dqa, dqb, dy, dx, do = chunk(
-            scal, first, queries, out_grad, query_other, grad_other, y, x, o, c0, nk, dqa
+            band_scal, first, queries, out_grad, query_other, grad_other, y, x, o, c0, nk, dqa, pair=4, mode=1
         )
         if parts:
             parts[-1], dx, dy = lax.optimization_barrier((parts[-1], dx, dy))

time: 85 us -> 91.2 us (1.073); the launches traced: 84.7 us -> 92.7 us
  starting transfers between devices: 21.1 us -> 25.4 us
  waiting for transfers between devices: 25.5 us -> 27.8 us
    ppermute x8, starting transfers between devices: 13.3 us -> 17.9 us  [rolled(): lax.ppermute(value, AXES, [(s, (s + steps) % count) for s in range(count)])]
    ppermute x8, waiting for transfers between devices: 24 us -> 26.2 us  [rolled(): lax.ppermute(value, AXES, [(s, (s + steps) % count) for s in range(count)])]
  transfers between devices with their start and end apart: 15 -> 15, of which waited for: 6 -> 6; matrix products, arithmetic and copies ran while one was open for 1% -> 1% of each run, Pallas kernels for 35% -> 33%
where the time goes in v1:
time: 91.2 us; the launch traced here: 92.7 us
  Pallas kernels  32.3 us (35%)
  waiting for transfers between devices  27.8 us (30%)
  starting transfers between devices  25.4 us (28%)
  local copies, waits for them, and re-layouts  4.94 us (5%)
  other arithmetic  1.26 us (1%)
  between operations  0.93 us (1%)
    pallas_call x2, Pallas kernels, chunk(): pl.pallas_call(functools.partial(kernel, pair=pair, mode=mode), grid_spec...  26.3 us
    ppermute x8, waiting for transfers between devices, rolled(): lax.ppermute(value, AXES, [(s, (s + steps) % count) for s in range(count)])  26.2 us
    ppermute x8, starting transfers between devices, rolled(): lax.ppermute(value, AXES, [(s, (s + steps) % count) for s in range(count)])  17.9 us
    ppermute x7, starting transfers between devices, core_swapped(): return lax.ppermute(value, AXES, [(s, s ^ 1) for s in range(count)])  7.52 us
    pallas_call x5, Pallas kernels, small_call(): pl.pallas_call(body, grid_spec=pltpu.PrefetchScalarGridSpec(num_scalar_pr...  6 us
    unnamed x8, local copies, waits for them, and re-layouts  4.83 us
  transfers between devices with their start and end apart: 15, of which 6 were waited for; matrix products, arithmetic and copies ran while one was open for 1% of the time, Pallas kernels for 33%

profile of v1, /device:TPU:1, one launch (start us, length us, event | category | flops | bytes accessed | tf_op | source)
XLA Modules:
  0.0 92.7 jit_solution(7070746856094767178)
XLA Ops:
  0.6 3.3 %collective-permute-start = (bf16[128,1024]{1,0:T(8,128)(2,1)}, bf16[128,1024]{1,0:T(8,128)(2,1)S(1)}, u32[]{:S(2)}, u32[]{:S(2)}) collective-permute-start(bf16[128,1024]{1,0:T(8,128)(2,1)} %km.1), channel_id=1, source_target_pairs={{0,1},{1,0},{2,3},{3,2},{4,5},{5,4},{6,7},{7,6},{8,9},{9,8},{10,11... | collective-permute-start | bytes 786440 | tf_op jit(solution)/shard_map/ppermute | solution.py:106
  4.0 0.1 collective-permute-start.1
  4.1 0.1 pad_add_fusion.s
  4.1 1.2 %collective-permute-done.kt = bf16[128,1024]{1,0:T(8,128)(2,1)S(1)} collective-permute-done((bf16[128,1024]{1,0:T(8,128)(2,1)}, bf16[128,1024]{1,0:T(8,128)(2,1)S(1)}, u32[]{:S(2)}, u32[]{:S(2)}) %collective-permute-start) | collective-permute-done | bytes 262176 | tf_op jit(solution)/shard_map/ppermute | solution.py:106
  5.3 0.4 collective-permute-done.1.vt
  5.7 0.0 copy-start
  5.7 0.9 %copy-done = bf16[128,1024]{1,0:T(8,128)(2,1)S(1)} copy-done((bf16[128,1024]{1,0:T(8,128)(2,1)S(1)}, bf16[128,1024]{1,0:T(8,128)(2,1)}, u32[]{:S(2)}) %copy-start) | copy-done | bytes 262168
  6.7 0.0 copy-start.1
  6.7 0.9 %copy-done.1 = bf16[128,1024]{1,0:T(8,128)(2,1)S(1)} copy-done((bf16[128,1024]{1,0:T(8,128)(2,1)S(1)}, bf16[128,1024]{1,0:T(8,128)(2,1)}, u32[]{:S(2)}) %copy-start.1) | copy-done | bytes 262168
  7.6 0.7 assemble.1
  8.3 0.5 collective-permute-start.2
  8.7 0.1 collective-permute-start.3
  8.9 0.1 add_multiply_fusion
  9.0 0.1 add_add_fusion
  9.0 0.9 fusion
  9.9 0.1 slice_reduce_fusion
  10.0 0.1 collective-permute-start.5
  10.1 0.8 collective-permute-start.4
  10.9 0.1 fusion.1
  11.0 0.1 pad_add_fusion.1.scal
  11.0 1.3 %collective-permute-start.8 = (bf16[256,512]{1,0:T(8,128)(2,1)S(1)}, bf16[256,512]{1,0:T(8,128)(2,1)S(1)}, u32[]{:S(2)}, u32[]{:S(2)}) collective-permute-start(bf16[256,512]{1,0:T(8,128)(2,1)S(1)} %get-tuple-element.38.o_ref), channel_id=1, source_target_pairs={{0,2},{1,3},{2,4},{3,5},{4,6},{5,7},{6,8},{7,9},{8,10},{9,11},{10,... | collective-permute-start | bytes 786440 | tf_op jit(solution)/shard_map/ppermute | solution.py:101
  12.3 16.0 %collective-permute-done.5.x_ref = bf16[256,512]{1,0:T(8,128)(2,1)S(1)} collective-permute-done((bf16[256,512]{1,0:T(8,128)(2,1)S(1)}, bf16[256,512]{1,0:T(8,128)(2,1)S(1)}, u32[]{:S(2)}, u32[]{:S(2)}) %collective-permute-start.5) | collective-permute-done | bytes 262176 | tf_op jit(solution)/shard_map/ppermute | solution.py:101
  28.3 0.0 collective-permute-start.7
  28.3 1.6 %collective-permute-done.4.y_ref = bf16[256,512]{1,0:T(8,128)(2,1)S(1)} collective-permute-done((bf16[256,512]{1,0:T(8,128)(2,1)S(1)}, bf16[256,512]{1,0:T(8,128)(2,1)S(1)}, u32[]{:S(2)}, u32[]{:S(2)}) %collective-permute-start.4) | collective-permute-done | bytes 262176 | tf_op jit(solution)/shard_map/ppermute | solution.py:101
  30.0 0.0 collective-permute-done.2.qb
  30.0 0.0 copy-start.3
  30.0 0.0 collective-permute-done.3.gb
  30.0 1.3 %copy-done.3 = bf16[128,8192]{1,0:T(8,128)(2,1)} copy-done((bf16[128,8192]{1,0:T(8,128)(2,1)}, bf16[128,8192]{1,0:T(8,128)(2,1)S(1)}, u32[]{:S(2)}) %copy-start.3) | copy-done | bytes 2097176
  31.3 0.0 copy-start.2
  31.3 1.6 %copy-done.2 = bf16[128,8192]{1,0:T(8,128)(2,1)S(1)} copy-done((bf16[128,8192]{1,0:T(8,128)(2,1)S(1)}, bf16[128,8192]{1,0:T(8,128)(2,1)}, u32[]{:S(2)}) %copy-start.2) | copy-done | bytes 2097176
  32.9 8.0 %band_grads.2 = (bf16[128,8192]{1,0:T(8,128)(2,1)}, bf16[128,2048]{1,0:T(8,128)(2,1)S(1)}, bf16[256,512]{1,0:T(8,128)(2,1)S(1)}, bf16[256,512]{1,0:T(8,128)(2,1)S(1)}, f32[256,512]{1,0:T(8,128)S(1)}) custom-call(s32[4]{0:T(128)S(1)} %pad_add_fusion.1.scal, s32[2,128]{1,0:T(2,128)S(1)} %broadcast_subtract_fusion.first_ref, bf16[128,8192]{1,0:T(8,128)(2,1)S(1)} %copy-done.2, ...), custom_call_target="tpu_custom_call" | custom-call | flops 13421772800 | bytes 4194304 | tf_op jit(solution)/shard_map/band_grads/pallas_call | solution.py:84
  40.9 4.4 %collective-permute-start.10 = (bf16[256,512]{1,0:T(8,128)(2,1)S(1)}, bf16[256,512]{1,0:T(8,128)(2,1)S(1)}, u32[]{:S(2)}, u32[]{:S(2)}) collective-permute-start(bf16[256,512]{1,0:T(8,128)(2,1)S(1)} %get-tuple-element.44), channel_id=1, source_target_pairs={{0,254},{1,255},{2,0},{3,1},{4,2},{5,3},{6,4},{7,5},{8,6},{9,7},{1... | collective-permute-start | bytes 786440 | tf_op jit(solution)/shard_map/ppermute | solution.py:101
  45.3 4.9 %collective-permute-start.11 = (bf16[256,512]{1,0:T(8,128)(2,1)S(1)}, bf16[256,512]{1,0:T(8,128)(2,1)S(1)}, u32[]{:S(2)}, u32[]{:S(2)}) collective-permute-start(bf16[256,512]{1,0:T(8,128)(2,1)S(1)} %get-tuple-element.45), channel_id=1, source_target_pairs={{0,252},{1,253},{2,254},{3,255},{4,0},{5,1},{6,2},{7,3},{8,4},{9,5... | collective-permute-start | bytes 786440 | tf_op jit(solution)/shard_map/ppermute | solution.py:101
  50.2 0.0 collective-permute-done.8.x_ref
  50.2 0.0 collective-permute-done.7.y_ref
  50.2 18.3 %band_grads.3 = (bf16[128,8192]{1,0:T(8,128)(2,1)}, bf16[128,2048]{1,0:T(8,128)(2,1)S(1)}, bf16[256,512]{1,0:T(8,128)(2,1)S(1)}, bf16[256,512]{1,0:T(8,128)(2,1)S(1)}, f32[256,512]{1,0:T(8,128)S(1)}) custom-call(s32[4]{0:T(128)S(1)} %pad_add_fusion.1.scal, s32[2,128]{1,0:T(2,128)S(1)} %broadcast_subtract_fusion.first_ref, ...), custom_call_target="tpu_custom_call", output_to_operand_aliasing={{0}: (9, {})} | custom-call | flops 13421772800 | bytes 4194304 | tf_op jit(solution)/shard_map/band_grads/pallas_call | solution.py:84
  68.5 0.0 collective-permute-done.10.x
  68.5 0.0 collective-permute-done.11.y
  68.5 6.5 %collective-permute-start.12 = (bf16[256,512]{1,0:T(8,128)(2,1)S(1)}, bf16[256,512]{1,0:T(8,128)(2,1)S(1)}, u32[]{:S(2)}, u32[]{:S(2)}) collective-permute-start(bf16[256,512]{1,0:T(8,128)(2,1)S(1)} %get-tuple-element.48), channel_id=1, source_target_pairs={{0,254},{1,255},{2,0},{3,1},{4,2},{5,3},{6,4},{7,5},{8,6},{9,7},{1... | collective-permute-start | bytes 786440 | tf_op jit(solution)/shard_map/ppermute | solution.py:101
  75.0 0.0 collective-permute-start.13
  75.0 1.4 %collective-permute-start.9 = (bf16[128,2048]{1,0:T(8,128)(2,1)S(1)}, bf16[128,2048]{1,0:T(8,128)(2,1)S(1)}, u32[]{:S(2)}, u32[]{:S(2)}) collective-permute-start(bf16[128,2048]{1,0:T(8,128)(2,1)S(1)} %get-tuple-element.40), channel_id=1, source_target_pairs={{0,1},{1,0},{2,3},{3,2},{4,5},{5,4},{6,7},{7,6},{8,9},{9,8},{10,11... | collective-permute-start | bytes 1572872 | tf_op jit(solution)/shard_map/ppermute | solution.py:106
  76.5 0.0 collective-permute-start.6
  76.5 1.2 %add_parts.2 = (bf16[128,1024]{1,0:T(8,128)(2,1)}, bf16[128,1024]{1,0:T(8,128)(2,1)}, bf16[128,1024]{1,0:T(8,128)(2,1)S(1)}) custom-call(s32[2]{0:T(128)S(1)} %pad_add_fusion.s, f32[256,512]{1,0:T(8,128)S(1)} %get-tuple-element.50.o, bf16[256,512]{1,0:T(8,128)(2,1)S(1)} %collective-permute-done.10.x, bf16[256,512]{1,0:T(8,128)(2,1)S(1)} %collective-permute-done.11.y), custom_call_target="tpu_custom_call" | custom-call | bytes 2097152 | tf_op jit(solution)/shard_map/add_parts/pallas_call | solution.py:110
  77.7 3.0 %collective-permute-done.12.x = bf16[256,512]{1,0:T(8,128)(2,1)S(1)} collective-permute-done((bf16[256,512]{1,0:T(8,128)(2,1)S(1)}, bf16[256,512]{1,0:T(8,128)(2,1)S(1)}, u32[]{:S(2)}, u32[]{:S(2)}) %collective-permute-start.12) | collective-permute-done | bytes 262176 | tf_op jit(solution)/shard_map/ppermute | solution.py:101
  80.7 5.6 %collective-permute-done.13.y = bf16[256,512]{1,0:T(8,128)(2,1)S(1)} collective-permute-done((bf16[256,512]{1,0:T(8,128)(2,1)S(1)}, bf16[256,512]{1,0:T(8,128)(2,1)S(1)}, u32[]{:S(2)}, u32[]{:S(2)}) %collective-permute-start.13) | collective-permute-done | bytes 262176 | tf_op jit(solution)/shard_map/ppermute | solution.py:101
  86.3 1.2 %add_parts.3 = (bf16[128,1024]{1,0:T(8,128)(2,1)}, bf16[128,1024]{1,0:T(8,128)(2,1)}, bf16[128,1024]{1,0:T(8,128)(2,1)S(1)}) custom-call(s32[2]{0:T(128)S(1)} %pad_add_fusion.s, f32[256,512]{1,0:T(8,128)S(1)} %get-tuple-element.42.o, bf16[256,512]{1,0:T(8,128)(2,1)S(1)} %collective-permute-done.12.x, ...), custom_call_target="tpu_custom_call", output_to_operand_aliasing={{0}: (4, {}), {1}: (5, {}), {2}: (6, {})} | custom-call | bytes 2097152 | tf_op jit(solution)/shard_map/add_parts/pallas_call | solution.py:110
  87.5 2.1 %collective-permute-start.14 = (bf16[128,1024]{1,0:T(8,128)(2,1)S(1)}, bf16[128,1024]{1,0:T(8,128)(2,1)S(1)}, u32[]{:S(2)}, u32[]{:S(2)}) collective-permute-start(bf16[128,1024]{1,0:T(8,128)(2,1)S(1)} %get-tuple-element.56), channel_id=1, source_target_pairs={{0,1},{1,0},{2,3},{3,2},{4,5},{5,4},{6,7},{7,6},{8,9},{9,8},{10,11... | collective-permute-start | bytes 786440 | tf_op jit(solution)/shard_map/ppermute | solution.py:106
  89.6 0.0 collective-permute-done.9.refs_1_
  89.6 0.0 collective-permute-done.6.refs_0_
  89.6 1.6 %place_query_grads.1 = bf16[128,8192]{1,0:T(8,128)(2,1)} custom-call(s32[2]{0:T(128)S(1)} %pad_add_fusion.s, bf16[128,2048]{1,0:T(8,128)(2,1)S(1)} %collective-permute-done.6.refs_0_, bf16[128,2048]{1,0:T(8,128)(2,1)S(1)} %collective-permute-done.9.refs_1_, bf16[128,8192]{1,0:T(8,128)(2,1)} %get-tuple-element.41.refs_2_), custom_call_target="tpu_custom_call", output_to_operand_aliasing={{}: (3, {})} | custom-call | bytes 2097152 | tf_op jit(solution)/shard_map/place_query_grads/pallas_call | solution.py:110
  91.2 0.0 collective-permute-done.14.b
  91.2 1.3 %place_key_grads.1 = (bf16[128,1024]{1,0:T(8,128)(2,1)}, bf16[128,1024]{1,0:T(8,128)(2,1)}) custom-call(s32[2]{0:T(128)S(1)} %pad_add_fusion.s, bf16[128,1024]{1,0:T(8,128)(2,1)S(1)} %collective-permute-done.14.b, bf16[128,1024]{1,0:T(8,128)(2,1)} %get-tuple-element.57.k_in, ...), custom_call_target="tpu_custom_call", output_to_operand_aliasing={{0}: (2, {}), {1}: (3, {})} | custom-call | bytes 524288 | tf_op jit(solution)/shard_map/place_key_grads/pallas_call | solution.py:110
  (1 shorter events, 0.0 us)
Async XLA Ops:
  0.6 4.7 %collective-permute-start = (bf16[128,1024]{1,0:T(8,128)(2,1)}, bf16[128,1024]{1,0:T(8,128)(2,1)S(1)}, u32[]{:S(2)}, u32[]{:S(2)}) collective-permute-start(bf16[128,1024]{1,0:T(8,128)(2,1)} %km.1), channel_id=1, source_target_pairs={{0,1},{1,0},{2,3},{3,2},{4,5},{5,4},{6,7},{7,6},{8,9},{9,8},{10,11... | collective-permute-start | bytes 786440 | tf_op jit(solution)/shard_map/ppermute | solution.py:106
  4.0 1.7 %collective-permute-start.1 = (bf16[128,1024]{1,0:T(8,128)(2,1)}, bf16[128,1024]{1,0:T(8,128)(2,1)S(1)}, u32[]{:S(2)}, u32[]{:S(2)}) collective-permute-start(bf16[128,1024]{1,0:T(8,128)(2,1)} %vm.1), channel_id=1, source_target_pairs={{0,1},{1,0},{2,3},{3,2},{4,5},{5,4},{6,7},{7,6},{8,9},{9,8},{10,11... | collective-permute-start | bytes 786440 | tf_op jit(solution)/shard_map/ppermute | solution.py:106
  5.7 0.9 %copy-start = (bf16[128,1024]{1,0:T(8,128)(2,1)S(1)}, bf16[128,1024]{1,0:T(8,128)(2,1)}, u32[]{:S(2)}) copy-start(bf16[128,1024]{1,0:T(8,128)(2,1)} %km.1) | copy-start | bytes 786436
  6.7 0.9 %copy-start.1 = (bf16[128,1024]{1,0:T(8,128)(2,1)S(1)}, bf16[128,1024]{1,0:T(8,128)(2,1)}, u32[]{:S(2)}) copy-start(bf16[128,1024]{1,0:T(8,128)(2,1)} %vm.1) | copy-start | bytes 786436
  8.3 21.7 %collective-permute-start.2 = (bf16[128,8192]{1,0:T(8,128)(2,1)}, bf16[128,8192]{1,0:T(8,128)(2,1)S(1)}, u32[]{:S(2)}, u32[]{:S(2)}) collective-permute-start(bf16[128,8192]{1,0:T(8,128)(2,1)} %qa.1), channel_id=1, source_target_pairs={{0,1},{1,0},{2,3},{3,2},{4,5},{5,4},{6,7},{7,6},{8,9},{9,8},{10,11... | collective-permute-start | bytes 6291464 | tf_op jit(solution)/shard_map/ppermute | solution.py:106
  8.7 21.2 %collective-permute-start.3 = (bf16[128,8192]{1,0:T(8,128)(2,1)}, bf16[128,8192]{1,0:T(8,128)(2,1)}, u32[]{:S(2)}, u32[]{:S(2)}) collective-permute-start(bf16[128,8192]{1,0:T(8,128)(2,1)} %ga.1), channel_id=1, source_target_pairs={{0,1},{1,0},{2,3},{3,2},{4,5},{5,4},{6,7},{7,6},{8,9},{9,8},{10,11... | collective-permute-start | bytes 6291464 | tf_op jit(solution)/shard_map/ppermute | solution.py:106
  10.0 18.3 %collective-permute-start.5 = (bf16[256,512]{1,0:T(8,128)(2,1)S(1)}, bf16[256,512]{1,0:T(8,128)(2,1)S(1)}, u32[]{:S(2)}, u32[]{:S(2)}) collective-permute-start(bf16[256,512]{1,0:T(8,128)(2,1)S(1)} %get-tuple-element.36.o_ref), channel_id=1, source_target_pairs={{0,2},{1,3},{2,4},{3,5},{4,6},{5,7},{6,8},{7,9},{8,10},{9,11},{10,... | collective-permute-start | bytes 786440 | tf_op jit(solution)/shard_map/ppermute | solution.py:101
  10.1 19.9 %collective-permute-start.4 = (bf16[256,512]{1,0:T(8,128)(2,1)S(1)}, bf16[256,512]{1,0:T(8,128)(2,1)S(1)}, u32[]{:S(2)}, u32[]{:S(2)}) collective-permute-start(bf16[256,512]{1,0:T(8,128)(2,1)S(1)} %get-tuple-element.36.o_ref), channel_id=1, source_target_pairs={{0,4},{1,5},{2,6},{3,7},{4,8},{5,9},{6,10},{7,11},{8,12},{9,13},{1... | collective-permute-start | bytes 786440 | tf_op jit(solution)/shard_map/ppermute | solution.py:101
  11.0 39.1 %collective-permute-start.8 = (bf16[256,512]{1,0:T(8,128)(2,1)S(1)}, bf16[256,512]{1,0:T(8,128)(2,1)S(1)}, u32[]{:S(2)}, u32[]{:S(2)}) collective-permute-start(bf16[256,512]{1,0:T(8,128)(2,1)S(1)} %get-tuple-element.38.o_ref), channel_id=1, source_target_pairs={{0,2},{1,3},{2,4},{3,5},{4,6},{5,7},{6,8},{7,9},{8,10},{9,11},{10,... | collective-permute-start | bytes 786440 | tf_op jit(solution)/shard_map/ppermute | solution.py:101
  28.3 21.8 %collective-permute-start.7 = (bf16[256,512]{1,0:T(8,128)(2,1)S(1)}, bf16[256,512]{1,0:T(8,128)(2,1)S(1)}, u32[]{:S(2)}, u32[]{:S(2)}) collective-permute-start(bf16[256,512]{1,0:T(8,128)(2,1)S(1)} %get-tuple-element.38.o_ref), channel_id=1, source_target_pairs={{0,4},{1,5},{2,6},{3,7},{4,8},{5,9},{6,10},{7,11},{8,12},{9,13},{1... | collective-permute-start | bytes 786440 | tf_op jit(solution)/shard_map/ppermute | solution.py:101
  30.0 1.3 %copy-start.3 = (bf16[128,8192]{1,0:T(8,128)(2,1)}, bf16[128,8192]{1,0:T(8,128)(2,1)S(1)}, u32[]{:S(2)}) copy-start(bf16[128,8192]{1,0:T(8,128)(2,1)S(1)} %collective-permute-done.2.qb) | copy-start | bytes 6291460
  31.3 1.6 %copy-start.2 = (bf16[128,8192]{1,0:T(8,128)(2,1)S(1)}, bf16[128,8192]{1,0:T(8,128)(2,1)}, u32[]{:S(2)}) copy-start(bf16[128,8192]{1,0:T(8,128)(2,1)} %qa.1) | copy-start | bytes 6291460
  40.9 27.6 %collective-permute-start.10 = (bf16[256,512]{1,0:T(8,128)(2,1)S(1)}, bf16[256,512]{1,0:T(8,128)(2,1)S(1)}, u32[]{:S(2)}, u32[]{:S(2)}) collective-permute-start(bf16[256,512]{1,0:T(8,128)(2,1)S(1)} %get-tuple-element.44), channel_id=1, source_target_pairs={{0,254},{1,255},{2,0},{3,1},{4,2},{5,3},{6,4},{7,5},{8,6},{9,7},{1... | collective-permute-start | bytes 786440 | tf_op jit(solution)/shard_map/ppermute | solution.py:101
  45.3 23.2 %collective-permute-start.11 = (bf16[256,512]{1,0:T(8,128)(2,1)S(1)}, bf16[256,512]{1,0:T(8,128)(2,1)S(1)}, u32[]{:S(2)}, u32[]{:S(2)}) collective-permute-start(bf16[256,512]{1,0:T(8,128)(2,1)S(1)} %get-tuple-element.45), channel_id=1, source_target_pairs={{0,252},{1,253},{2,254},{3,255},{4,0},{5,1},{6,2},{7,3},{8,4},{9,5... | collective-permute-start | bytes 786440 | tf_op jit(solution)/shard_map/ppermute | solution.py:101
  68.5 12.2 %collective-permute-start.12 = (bf16[256,512]{1,0:T(8,128)(2,1)S(1)}, bf16[256,512]{1,0:T(8,128)(2,1)S(1)}, u32[]{:S(2)}, u32[]{:S(2)}) collective-permute-start(bf16[256,512]{1,0:T(8,128)(2,1)S(1)} %get-tuple-element.48), channel_id=1, source_target_pairs={{0,254},{1,255},{2,0},{3,1},{4,2},{5,3},{6,4},{7,5},{8,6},{9,7},{1... | collective-permute-start | bytes 786440 | tf_op jit(solution)/shard_map/ppermute | solution.py:101
  75.0 11.3 %collective-permute-start.13 = (bf16[256,512]{1,0:T(8,128)(2,1)S(1)}, bf16[256,512]{1,0:T(8,128)(2,1)S(1)}, u32[]{:S(2)}, u32[]{:S(2)}) collective-permute-start(bf16[256,512]{1,0:T(8,128)(2,1)S(1)} %get-tuple-element.49), channel_id=1, source_target_pairs={{0,252},{1,253},{2,254},{3,255},{4,0},{5,1},{6,2},{7,3},{8,4},{9,5... | collective-permute-start | bytes 786440 | tf_op jit(solution)/shard_map/ppermute | solution.py:101
  75.0 14.6 %collective-permute-start.9 = (bf16[128,2048]{1,0:T(8,128)(2,1)S(1)}, bf16[128,2048]{1,0:T(8,128)(2,1)S(1)}, u32[]{:S(2)}, u32[]{:S(2)}) collective-permute-start(bf16[128,2048]{1,0:T(8,128)(2,1)S(1)} %get-tuple-element.40), channel_id=1, source_target_pairs={{0,1},{1,0},{2,3},{3,2},{4,5},{5,4},{6,7},{7,6},{8,9},{9,8},{10,11... | collective-permute-start | bytes 1572872 | tf_op jit(solution)/shard_map/ppermute | solution.py:106
  76.5 13.2 %collective-permute-start.6 = (bf16[128,2048]{1,0:T(8,128)(2,1)S(1)}, bf16[128,2048]{1,0:T(8,128)(2,1)S(1)}, u32[]{:S(2)}, u32[]{:S(2)}) collective-permute-start(bf16[128,2048]{1,0:T(8,128)(2,1)S(1)} %get-tuple-element.37), channel_id=1, source_target_pairs={{0,1},{1,0},{2,3},{3,2},{4,5},{5,4},{6,7},{7,6},{8,9},{9,8},{10,11... | collective-permute-start | bytes 1572872 | tf_op jit(solution)/shard_map/ppermute | solution.py:106
  87.5 3.7 %collective-permute-start.14 = (bf16[128,1024]{1,0:T(8,128)(2,1)S(1)}, bf16[128,1024]{1,0:T(8,128)(2,1)S(1)}, u32[]{:S(2)}, u32[]{:S(2)}) collective-permute-start(bf16[128,1024]{1,0:T(8,128)(2,1)S(1)} %get-tuple-element.56), channel_id=1, source_target_pairs={{0,1},{1,0},{2,3},{3,2},{4,5},{5,4},{6,7},{7,6},{8,9},{9,8},{10,11... | collective-permute-start | bytes 786440 | tf_op jit(solution)/shard_map/ppermute | solution.py:106

commit v2 on v1

--- a/solution.py
+++ b/solution.py
@@ -225,6 +225,9 @@
     queries, out_grad, own = lax.optimization_barrier((queries, out_grad, tuple(own)))
     query_other = core_swapped(queries)
     grad_other = core_swapped(out_grad)
+    doc_starts, query_other, grad_other = lax.optimization_barrier(
+        (doc_starts, query_other, grad_other)
+    )
     rows = jnp.stack([core, 1 - core])[:, None] * BLK + jnp.arange(BLK)[None, :] + chip * 256
     reached = jnp.where(doc_starts[None, None, :] <= rows[:, :, None], doc_starts[None, None, :], 0)
     first = jnp.max(reached, axis=-1) - (chip * 256 - 512)

time: 91.2 us -> 89.2 us (0.978); the launches traced: 92.7 us -> 88.2 us
  waiting for transfers between devices: 27.8 us -> 25.4 us
  local copies, waits for them, and re-layouts: 4.94 us -> 3.61 us
    ppermute x8, waiting for transfers between devices: 26.2 us -> 19 us  [rolled(): lax.ppermute(value, AXES, [(s, (s + steps) % count) for s in range(count)])]
    ppermute x7, waiting for transfers between devices: 1.58 us -> 6.37 us  [core_swapped(): return lax.ppermute(value, AXES, [(s, s ^ 1) for s in range(count)])]
    unnamed x8, local copies, waits for them, and re-layouts: 4.83 us -> 3.49 us
  transfers between devices with their start and end apart: 15 -> 15, of which waited for: 6 -> 8; matrix products, arithmetic and copies ran while one was open for 1% -> 2% of each run, Pallas kernels for 33% -> 34%
where the time goes in v2:
time: 89.2 us; the launch traced here: 88.2 us
  Pallas kernels  32.3 us (36%)
  waiting for transfers between devices  25.4 us (28%)
  starting transfers between devices  24.7 us (28%)
  local copies, waits for them, and re-layouts  3.61 us (4%)
  other arithmetic  1.26 us (1%)
  between operations  0.93 us (1%)
    pallas_call x2, Pallas kernels, chunk(): pl.pallas_call(functools.partial(kernel, pair=pair, mode=mode), grid_spec...  26.3 us
    ppermute x8, waiting for transfers between devices, rolled(): lax.ppermute(value, AXES, [(s, (s + steps) % count) for s in range(count)])  19 us
    ppermute x8, starting transfers between devices, rolled(): lax.ppermute(value, AXES, [(s, (s + steps) % count) for s in range(count)])  17.1 us
    ppermute x7, starting transfers between devices, core_swapped(): return lax.ppermute(value, AXES, [(s, s ^ 1) for s in range(count)])  7.6 us
    ppermute x7, waiting for transfers between devices, core_swapped(): return lax.ppermute(value, AXES, [(s, s ^ 1) for s in range(count)])  6.37 us
    pallas_call x5, Pallas kernels, small_call(): pl.pallas_call(body, grid_spec=pltpu.PrefetchScalarGridSpec(num_scalar_pr...  6.01 us
    unnamed x8, local copies, waits for them, and re-layouts  3.49 us
  transfers between devices with their start and end apart: 15, of which 8 were waited for; matrix products, arithmetic and copies ran while one was open for 2% of the time, Pallas kernels for 34%

profile of v2, /device:TPU:1, one launch (start us, length us, event | category | flops | bytes accessed | tf_op | source)
XLA Modules:
  0.0 88.2 jit_solution(7959648688962298214)
XLA Ops:
  0.6 3.3 %collective-permute-start = (bf16[128,1024]{1,0:T(8,128)(2,1)}, bf16[128,1024]{1,0:T(8,128)(2,1)S(1)}, u32[]{:S(2)}, u32[]{:S(2)}) collective-permute-start(bf16[128,1024]{1,0:T(8,128)(2,1)} %km.1), channel_id=1, source_target_pairs={{0,1},{1,0},{2,3},{3,2},{4,5},{5,4},{6,7},{7,6},{8,9},{9,8},{10,11... | collective-permute-start | bytes 786440 | tf_op jit(solution)/shard_map/ppermute | solution.py:106
  4.0 0.1 collective-permute-start.1
  4.1 0.1 pad_add_fusion.s
  4.1 1.2 %collective-permute-done.kt = bf16[128,1024]{1,0:T(8,128)(2,1)S(1)} collective-permute-done((bf16[128,1024]{1,0:T(8,128)(2,1)}, bf16[128,1024]{1,0:T(8,128)(2,1)S(1)}, u32[]{:S(2)}, u32[]{:S(2)}) %collective-permute-start) | collective-permute-done | bytes 262176 | tf_op jit(solution)/shard_map/ppermute | solution.py:106
  5.3 0.4 collective-permute-done.1.vt
  5.7 0.0 copy-start
  5.7 0.9 %copy-done = bf16[128,1024]{1,0:T(8,128)(2,1)S(1)} copy-done((bf16[128,1024]{1,0:T(8,128)(2,1)S(1)}, bf16[128,1024]{1,0:T(8,128)(2,1)}, u32[]{:S(2)}) %copy-start) | copy-done | bytes 262168
  6.7 0.0 copy-start.1
  6.7 0.9 %copy-done.1 = bf16[128,1024]{1,0:T(8,128)(2,1)S(1)} copy-done((bf16[128,1024]{1,0:T(8,128)(2,1)S(1)}, bf16[128,1024]{1,0:T(8,128)(2,1)}, u32[]{:S(2)}) %copy-start.1) | copy-done | bytes 262168
  7.6 0.7 assemble.1
  8.3 0.5 collective-permute-start.2
  8.7 0.1 collective-permute-start.3
  8.9 0.1 add_multiply_fusion
  9.0 0.1 add_add_fusion
  9.0 0.0 collective-permute-start.5
  9.0 0.8 collective-permute-start.4
  9.8 1.3 %collective-permute-start.8 = (bf16[256,512]{1,0:T(8,128)(2,1)S(1)}, bf16[256,512]{1,0:T(8,128)(2,1)S(1)}, u32[]{:S(2)}, u32[]{:S(2)}) collective-permute-start(bf16[256,512]{1,0:T(8,128)(2,1)S(1)} %get-tuple-element.44.o_ref), channel_id=1, source_target_pairs={{0,2},{1,3},{2,4},{3,5},{4,6},{5,7},{6,8},{7,9},{8,10},{9,11},{10,... | collective-permute-start | bytes 786440 | tf_op jit(solution)/shard_map/ppermute | solution.py:101
  11.1 3.3 %collective-permute-done.2.qb = bf16[128,8192]{1,0:T(8,128)(2,1)S(1)} collective-permute-done((bf16[128,8192]{1,0:T(8,128)(2,1)}, bf16[128,8192]{1,0:T(8,128)(2,1)S(1)}, u32[]{:S(2)}, u32[]{:S(2)}) %collective-permute-start.2) | collective-permute-done | bytes 2097184 | tf_op jit(solution)/shard_map/ppermute | solution.py:106
  14.4 0.0 copy-start.3
  14.4 0.0 collective-permute-start.7
  14.4 1.5 %collective-permute-done.3.gb = bf16[128,8192]{1,0:T(8,128)(2,1)} collective-permute-done((bf16[128,8192]{1,0:T(8,128)(2,1)}, bf16[128,8192]{1,0:T(8,128)(2,1)}, u32[]{:S(2)}, u32[]{:S(2)}) %collective-permute-start.3) | collective-permute-done | bytes 2097184 | tf_op jit(solution)/shard_map/ppermute | solution.py:106
  15.9 0.9 fusion
  16.7 0.1 slice_reduce_fusion
  16.9 0.1 fusion.1
  17.0 0.1 pad_add_fusion.1.scal
  17.0 10.2 %collective-permute-done.5.x_ref = bf16[256,512]{1,0:T(8,128)(2,1)S(1)} collective-permute-done((bf16[256,512]{1,0:T(8,128)(2,1)S(1)}, bf16[256,512]{1,0:T(8,128)(2,1)S(1)}, u32[]{:S(2)}, u32[]{:S(2)}) %collective-permute-start.5) | collective-permute-done | bytes 262176 | tf_op jit(solution)/shard_map/ppermute | solution.py:101
  27.3 1.6 %collective-permute-done.4.y_ref = bf16[256,512]{1,0:T(8,128)(2,1)S(1)} collective-permute-done((bf16[256,512]{1,0:T(8,128)(2,1)S(1)}, bf16[256,512]{1,0:T(8,128)(2,1)S(1)}, u32[]{:S(2)}, u32[]{:S(2)}) %collective-permute-start.4) | collective-permute-done | bytes 262176 | tf_op jit(solution)/shard_map/ppermute | solution.py:101
  28.9 0.0 copy-done.3
  28.9 0.0 copy-start.2
  28.9 1.6 %copy-done.2 = bf16[128,8192]{1,0:T(8,128)(2,1)S(1)} copy-done((bf16[128,8192]{1,0:T(8,128)(2,1)S(1)}, bf16[128,8192]{1,0:T(8,128)(2,1)}, u32[]{:S(2)}) %copy-start.2) | copy-done | bytes 2097176
  30.5 8.0 %band_grads.2 = (bf16[128,8192]{1,0:T(8,128)(2,1)}, bf16[128,2048]{1,0:T(8,128)(2,1)S(1)}, bf16[256,512]{1,0:T(8,128)(2,1)S(1)}, bf16[256,512]{1,0:T(8,128)(2,1)S(1)}, f32[256,512]{1,0:T(8,128)S(1)}) custom-call(s32[4]{0:T(128)S(1)} %pad_add_fusion.1.scal, s32[2,128]{1,0:T(2,128)S(1)} %broadcast_subtract_fusion.first_ref, bf16[128,8192]{1,0:T(8,128)(2,1)S(1)} %copy-done.2, ...), custom_call_target="tpu_custom_call" | custom-call | flops 13421772800 | bytes 4194304 | tf_op jit(solution)/shard_map/band_grads/pallas_call | solution.py:84
  38.5 4.4 %collective-permute-start.10 = (bf16[256,512]{1,0:T(8,128)(2,1)S(1)}, bf16[256,512]{1,0:T(8,128)(2,1)S(1)}, u32[]{:S(2)}, u32[]{:S(2)}) collective-permute-start(bf16[256,512]{1,0:T(8,128)(2,1)S(1)} %get-tuple-element.50), channel_id=1, source_target_pairs={{0,254},{1,255},{2,0},{3,1},{4,2},{5,3},{6,4},{7,5},{8,6},{9,7},{1... | collective-permute-start | bytes 786440 | tf_op jit(solution)/shard_map/ppermute | solution.py:101
  42.9 5.9 %collective-permute-start.11 = (bf16[256,512]{1,0:T(8,128)(2,1)S(1)}, bf16[256,512]{1,0:T(8,128)(2,1)S(1)}, u32[]{:S(2)}, u32[]{:S(2)}) collective-permute-start(bf16[256,512]{1,0:T(8,128)(2,1)S(1)} %get-tuple-element.51), channel_id=1, source_target_pairs={{0,252},{1,253},{2,254},{3,255},{4,0},{5,1},{6,2},{7,3},{8,4},{9,5... | collective-permute-start | bytes 786440 | tf_op jit(solution)/shard_map/ppermute | solution.py:101
  48.8 0.0 collective-permute-done.8.x_ref
  48.8 0.0 collective-permute-done.7.y_ref
  48.8 18.3 %band_grads.3 = (bf16[128,8192]{1,0:T(8,128)(2,1)}, bf16[128,2048]{1,0:T(8,128)(2,1)S(1)}, bf16[256,512]{1,0:T(8,128)(2,1)S(1)}, bf16[256,512]{1,0:T(8,128)(2,1)S(1)}, f32[256,512]{1,0:T(8,128)S(1)}) custom-call(s32[4]{0:T(128)S(1)} %pad_add_fusion.1.scal, s32[2,128]{1,0:T(2,128)S(1)} %broadcast_subtract_fusion.first_ref, ...), custom_call_target="tpu_custom_call", output_to_operand_aliasing={{0}: (9, {})} | custom-call | flops 13421772800 | bytes 4194304 | tf_op jit(solution)/shard_map/band_grads/pallas_call | solution.py:84
  67.1 0.0 collective-permute-done.10.x
  67.1 0.0 collective-permute-done.11.y
  67.1 3.2 %collective-permute-start.12 = (bf16[256,512]{1,0:T(8,128)(2,1)S(1)}, bf16[256,512]{1,0:T(8,128)(2,1)S(1)}, u32[]{:S(2)}, u32[]{:S(2)}) collective-permute-start(bf16[256,512]{1,0:T(8,128)(2,1)S(1)} %get-tuple-element.54), channel_id=1, source_target_pairs={{0,254},{1,255},{2,0},{3,1},{4,2},{5,3},{6,4},{7,5},{8,6},{9,7},{1... | collective-permute-start | bytes 786440 | tf_op jit(solution)/shard_map/ppermute | solution.py:101
  70.4 1.5 %collective-permute-start.13 = (bf16[256,512]{1,0:T(8,128)(2,1)S(1)}, bf16[256,512]{1,0:T(8,128)(2,1)S(1)}, u32[]{:S(2)}, u32[]{:S(2)}) collective-permute-start(bf16[256,512]{1,0:T(8,128)(2,1)S(1)} %get-tuple-element.55), channel_id=1, source_target_pairs={{0,252},{1,253},{2,254},{3,255},{4,0},{5,1},{6,2},{7,3},{8,4},{9,5... | collective-permute-start | bytes 786440 | tf_op jit(solution)/shard_map/ppermute | solution.py:101
  71.9 1.7 %collective-permute-start.9 = (bf16[128,2048]{1,0:T(8,128)(2,1)S(1)}, bf16[128,2048]{1,0:T(8,128)(2,1)S(1)}, u32[]{:S(2)}, u32[]{:S(2)}) collective-permute-start(bf16[128,2048]{1,0:T(8,128)(2,1)S(1)} %get-tuple-element.46), channel_id=1, source_target_pairs={{0,1},{1,0},{2,3},{3,2},{4,5},{5,4},{6,7},{7,6},{8,9},{9,8},{10,11... | collective-permute-start | bytes 1572872 | tf_op jit(solution)/shard_map/ppermute | solution.py:106
  73.6 0.0 collective-permute-start.6
  73.6 1.2 %add_parts.2 = (bf16[128,1024]{1,0:T(8,128)(2,1)}, bf16[128,1024]{1,0:T(8,128)(2,1)}, bf16[128,1024]{1,0:T(8,128)(2,1)S(1)}) custom-call(s32[2]{0:T(128)S(1)} %pad_add_fusion.s, f32[256,512]{1,0:T(8,128)S(1)} %get-tuple-element.56.o, bf16[256,512]{1,0:T(8,128)(2,1)S(1)} %collective-permute-done.10.x, bf16[256,512]{1,0:T(8,128)(2,1)S(1)} %collective-permute-done.11.y), custom_call_target="tpu_custom_call" | custom-call | bytes 2097152 | tf_op jit(solution)/shard_map/add_parts/pallas_call | solution.py:110
  74.8 4.2 %collective-permute-done.12.x = bf16[256,512]{1,0:T(8,128)(2,1)S(1)} collective-permute-done((bf16[256,512]{1,0:T(8,128)(2,1)S(1)}, bf16[256,512]{1,0:T(8,128)(2,1)S(1)}, u32[]{:S(2)}, u32[]{:S(2)}) %collective-permute-start.12) | collective-permute-done | bytes 262176 | tf_op jit(solution)/shard_map/ppermute | solution.py:101
  79.1 2.9 %collective-permute-done.13.y = bf16[256,512]{1,0:T(8,128)(2,1)S(1)} collective-permute-done((bf16[256,512]{1,0:T(8,128)(2,1)S(1)}, bf16[256,512]{1,0:T(8,128)(2,1)S(1)}, u32[]{:S(2)}, u32[]{:S(2)}) %collective-permute-start.13) | collective-permute-done | bytes 262176 | tf_op jit(solution)/shard_map/ppermute | solution.py:101
  81.9 1.2 %add_parts.3 = (bf16[128,1024]{1,0:T(8,128)(2,1)}, bf16[128,1024]{1,0:T(8,128)(2,1)}, bf16[128,1024]{1,0:T(8,128)(2,1)S(1)}) custom-call(s32[2]{0:T(128)S(1)} %pad_add_fusion.s, f32[256,512]{1,0:T(8,128)S(1)} %get-tuple-element.48.o, bf16[256,512]{1,0:T(8,128)(2,1)S(1)} %collective-permute-done.12.x, ...), custom_call_target="tpu_custom_call", output_to_operand_aliasing={{0}: (4, {}), {1}: (5, {}), {2}: (6, {})} | custom-call | bytes 2097152 | tf_op jit(solution)/shard_map/add_parts/pallas_call | solution.py:110
  83.2 1.9 %collective-permute-start.14 = (bf16[128,1024]{1,0:T(8,128)(2,1)S(1)}, bf16[128,1024]{1,0:T(8,128)(2,1)S(1)}, u32[]{:S(2)}, u32[]{:S(2)}) collective-permute-start(bf16[128,1024]{1,0:T(8,128)(2,1)S(1)} %get-tuple-element.62), channel_id=1, source_target_pairs={{0,1},{1,0},{2,3},{3,2},{4,5},{5,4},{6,7},{7,6},{8,9},{9,8},{10,11... | collective-permute-start | bytes 786440 | tf_op jit(solution)/shard_map/ppermute | solution.py:106
  85.1 0.0 collective-permute-done.9.refs_1_
  85.1 0.0 collective-permute-done.6.refs_0_
  85.1 1.6 %place_query_grads.1 = bf16[128,8192]{1,0:T(8,128)(2,1)} custom-call(s32[2]{0:T(128)S(1)} %pad_add_fusion.s, bf16[128,2048]{1,0:T(8,128)(2,1)S(1)} %collective-permute-done.6.refs_0_, bf16[128,2048]{1,0:T(8,128)(2,1)S(1)} %collective-permute-done.9.refs_1_, bf16[128,8192]{1,0:T(8,128)(2,1)} %get-tuple-element.47.refs_2_), custom_call_target="tpu_custom_call", output_to_operand_aliasing={{}: (3, {})} | custom-call | bytes 2097152 | tf_op jit(solution)/shard_map/place_query_grads/pallas_call | solution.py:110
  86.6 0.0 collective-permute-done.14.b
  86.6 1.3 %place_key_grads.1 = (bf16[128,1024]{1,0:T(8,128)(2,1)}, bf16[128,1024]{1,0:T(8,128)(2,1)}) custom-call(s32[2]{0:T(128)S(1)} %pad_add_fusion.s, bf16[128,1024]{1,0:T(8,128)(2,1)S(1)} %collective-permute-done.14.b, bf16[128,1024]{1,0:T(8,128)(2,1)} %get-tuple-element.63.k_in, ...), custom_call_target="tpu_custom_call", output_to_operand_aliasing={{0}: (2, {}), {1}: (3, {})} | custom-call | bytes 524288 | tf_op jit(solution)/shard_map/place_key_grads/pallas_call | solution.py:110
  (1 shorter events, 0.0 us)
Async XLA Ops:
  0.6 4.7 %collective-permute-start = (bf16[128,1024]{1,0:T(8,128)(2,1)}, bf16[128,1024]{1,0:T(8,128)(2,1)S(1)}, u32[]{:S(2)}, u32[]{:S(2)}) collective-permute-start(bf16[128,1024]{1,0:T(8,128)(2,1)} %km.1), channel_id=1, source_target_pairs={{0,1},{1,0},{2,3},{3,2},{4,5},{5,4},{6,7},{7,6},{8,9},{9,8},{10,11... | collective-permute-start | bytes 786440 | tf_op jit(solution)/shard_map/ppermute | solution.py:106
  4.0 1.7 %collective-permute-start.1 = (bf16[128,1024]{1,0:T(8,128)(2,1)}, bf16[128,1024]{1,0:T(8,128)(2,1)S(1)}, u32[]{:S(2)}, u32[]{:S(2)}) collective-permute-start(bf16[128,1024]{1,0:T(8,128)(2,1)} %vm.1), channel_id=1, source_target_pairs={{0,1},{1,0},{2,3},{3,2},{4,5},{5,4},{6,7},{7,6},{8,9},{9,8},{10,11... | collective-permute-start | bytes 786440 | tf_op jit(solution)/shard_map/ppermute | solution.py:106
  5.7 0.9 %copy-start = (bf16[128,1024]{1,0:T(8,128)(2,1)S(1)}, bf16[128,1024]{1,0:T(8,128)(2,1)}, u32[]{:S(2)}) copy-start(bf16[128,1024]{1,0:T(8,128)(2,1)} %km.1) | copy-start | bytes 786436
  6.7 0.9 %copy-start.1 = (bf16[128,1024]{1,0:T(8,128)(2,1)S(1)}, bf16[128,1024]{1,0:T(8,128)(2,1)}, u32[]{:S(2)}) copy-start(bf16[128,1024]{1,0:T(8,128)(2,1)} %vm.1) | copy-start | bytes 786436
  8.3 6.1 %collective-permute-start.2 = (bf16[128,8192]{1,0:T(8,128)(2,1)}, bf16[128,8192]{1,0:T(8,128)(2,1)S(1)}, u32[]{:S(2)}, u32[]{:S(2)}) collective-permute-start(bf16[128,8192]{1,0:T(8,128)(2,1)} %qa.1), channel_id=1, source_target_pairs={{0,1},{1,0},{2,3},{3,2},{4,5},{5,4},{6,7},{7,6},{8,9},{9,8},{10,11... | collective-permute-start | bytes 6291464 | tf_op jit(solution)/shard_map/ppermute | solution.py:106
  8.7 7.1 %collective-permute-start.3 = (bf16[128,8192]{1,0:T(8,128)(2,1)}, bf16[128,8192]{1,0:T(8,128)(2,1)}, u32[]{:S(2)}, u32[]{:S(2)}) collective-permute-start(bf16[128,8192]{1,0:T(8,128)(2,1)} %ga.1), channel_id=1, source_target_pairs={{0,1},{1,0},{2,3},{3,2},{4,5},{5,4},{6,7},{7,6},{8,9},{9,8},{10,11... | collective-permute-start | bytes 6291464 | tf_op jit(solution)/shard_map/ppermute | solution.py:106
  9.0 18.2 %collective-permute-start.5 = (bf16[256,512]{1,0:T(8,128)(2,1)S(1)}, bf16[256,512]{1,0:T(8,128)(2,1)S(1)}, u32[]{:S(2)}, u32[]{:S(2)}) collective-permute-start(bf16[256,512]{1,0:T(8,128)(2,1)S(1)} %get-tuple-element.42.o_ref), channel_id=1, source_target_pairs={{0,2},{1,3},{2,4},{3,5},{4,6},{5,7},{6,8},{7,9},{8,10},{9,11},{10,... | collective-permute-start | bytes 786440 | tf_op jit(solution)/shard_map/ppermute | solution.py:101
  9.0 19.9 %collective-permute-start.4 = (bf16[256,512]{1,0:T(8,128)(2,1)S(1)}, bf16[256,512]{1,0:T(8,128)(2,1)S(1)}, u32[]{:S(2)}, u32[]{:S(2)}) collective-permute-start(bf16[256,512]{1,0:T(8,128)(2,1)S(1)} %get-tuple-element.42.o_ref), channel_id=1, source_target_pairs={{0,4},{1,5},{2,6},{3,7},{4,8},{5,9},{6,10},{7,11},{8,12},{9,13},{1... | collective-permute-start | bytes 786440 | tf_op jit(solution)/shard_map/ppermute | solution.py:101
  9.8 39.0 %collective-permute-start.8 = (bf16[256,512]{1,0:T(8,128)(2,1)S(1)}, bf16[256,512]{1,0:T(8,128)(2,1)S(1)}, u32[]{:S(2)}, u32[]{:S(2)}) collective-permute-start(bf16[256,512]{1,0:T(8,128)(2,1)S(1)} %get-tuple-element.44.o_ref), channel_id=1, source_target_pairs={{0,2},{1,3},{2,4},{3,5},{4,6},{5,7},{6,8},{7,9},{8,10},{9,11},{10,... | collective-permute-start | bytes 786440 | tf_op jit(solution)/shard_map/ppermute | solution.py:101
  14.4 14.5 %copy-start.3 = (bf16[128,8192]{1,0:T(8,128)(2,1)}, bf16[128,8192]{1,0:T(8,128)(2,1)S(1)}, u32[]{:S(2)}) copy-start(bf16[128,8192]{1,0:T(8,128)(2,1)S(1)} %collective-permute-done.2.qb) | copy-start | bytes 6291460
  14.4 34.4 %collective-permute-start.7 = (bf16[256,512]{1,0:T(8,128)(2,1)S(1)}, bf16[256,512]{1,0:T(8,128)(2,1)S(1)}, u32[]{:S(2)}, u32[]{:S(2)}) collective-permute-start(bf16[256,512]{1,0:T(8,128)(2,1)S(1)} %get-tuple-element.44.o_ref), channel_id=1, source_target_pairs={{0,4},{1,5},{2,6},{3,7},{4,8},{5,9},{6,10},{7,11},{8,12},{9,13},{1... | collective-permute-start | bytes 786440 | tf_op jit(solution)/shard_map/ppermute | solution.py:101
  28.9 1.6 %copy-start.2 = (bf16[128,8192]{1,0:T(8,128)(2,1)S(1)}, bf16[128,8192]{1,0:T(8,128)(2,1)}, u32[]{:S(2)}) copy-start(bf16[128,8192]{1,0:T(8,128)(2,1)} %qa.1) | copy-start | bytes 6291460
  38.5 28.6 %collective-permute-start.10 = (bf16[256,512]{1,0:T(8,128)(2,1)S(1)}, bf16[256,512]{1,0:T(8,128)(2,1)S(1)}, u32[]{:S(2)}, u32[]{:S(2)}) collective-permute-start(bf16[256,512]{1,0:T(8,128)(2,1)S(1)} %get-tuple-element.50), channel_id=1, source_target_pairs={{0,254},{1,255},{2,0},{3,1},{4,2},{5,3},{6,4},{7,5},{8,6},{9,7},{1... | collective-permute-start | bytes 786440 | tf_op jit(solution)/shard_map/ppermute | solution.py:101
  42.9 24.2 %collective-permute-start.11 = (bf16[256,512]{1,0:T(8,128)(2,1)S(1)}, bf16[256,512]{1,0:T(8,128)(2,1)S(1)}, u32[]{:S(2)}, u32[]{:S(2)}) collective-permute-start(bf16[256,512]{1,0:T(8,128)(2,1)S(1)} %get-tuple-element.51), channel_id=1, source_target_pairs={{0,252},{1,253},{2,254},{3,255},{4,0},{5,1},{6,2},{7,3},{8,4},{9,5... | collective-permute-start | bytes 786440 | tf_op jit(solution)/shard_map/ppermute | solution.py:101
  67.1 11.9 %collective-permute-start.12 = (bf16[256,512]{1,0:T(8,128)(2,1)S(1)}, bf16[256,512]{1,0:T(8,128)(2,1)S(1)}, u32[]{:S(2)}, u32[]{:S(2)}) collective-permute-start(bf16[256,512]{1,0:T(8,128)(2,1)S(1)} %get-tuple-element.54), channel_id=1, source_target_pairs={{0,254},{1,255},{2,0},{3,1},{4,2},{5,3},{6,4},{7,5},{8,6},{9,7},{1... | collective-permute-start | bytes 786440 | tf_op jit(solution)/shard_map/ppermute | solution.py:101
  70.4 11.6 %collective-permute-start.13 = (bf16[256,512]{1,0:T(8,128)(2,1)S(1)}, bf16[256,512]{1,0:T(8,128)(2,1)S(1)}, u32[]{:S(2)}, u32[]{:S(2)}) collective-permute-start(bf16[256,512]{1,0:T(8,128)(2,1)S(1)} %get-tuple-element.55), channel_id=1, source_target_pairs={{0,252},{1,253},{2,254},{3,255},{4,0},{5,1},{6,2},{7,3},{8,4},{9,5... | collective-permute-start | bytes 786440 | tf_op jit(solution)/shard_map/ppermute | solution.py:101
  71.9 13.2 %collective-permute-start.9 = (bf16[128,2048]{1,0:T(8,128)(2,1)S(1)}, bf16[128,2048]{1,0:T(8,128)(2,1)S(1)}, u32[]{:S(2)}, u32[]{:S(2)}) collective-permute-start(bf16[128,2048]{1,0:T(8,128)(2,1)S(1)} %get-tuple-element.46), channel_id=1, source_target_pairs={{0,1},{1,0},{2,3},{3,2},{4,5},{5,4},{6,7},{7,6},{8,9},{9,8},{10,11... | collective-permute-start | bytes 1572872 | tf_op jit(solution)/shard_map/ppermute | solution.py:106
  73.6 11.5 %collective-permute-start.6 = (bf16[128,2048]{1,0:T(8,128)(2,1)S(1)}, bf16[128,2048]{1,0:T(8,128)(2,1)S(1)}, u32[]{:S(2)}, u32[]{:S(2)}) collective-permute-start(bf16[128,2048]{1,0:T(8,128)(2,1)S(1)} %get-tuple-element.43), channel_id=1, source_target_pairs={{0,1},{1,0},{2,3},{3,2},{4,5},{5,4},{6,7},{7,6},{8,9},{9,8},{10,11... | collective-permute-start | bytes 1572872 | tf_op jit(solution)/shard_map/ppermute | solution.py:106
  83.2 3.5 %collective-permute-start.14 = (bf16[128,1024]{1,0:T(8,128)(2,1)S(1)}, bf16[128,1024]{1,0:T(8,128)(2,1)S(1)}, u32[]{:S(2)}, u32[]{:S(2)}) collective-permute-start(bf16[128,1024]{1,0:T(8,128)(2,1)S(1)} %get-tuple-element.62), channel_id=1, source_target_pairs={{0,1},{1,0},{2,3},{3,2},{4,5},{5,4},{6,7},{7,6},{8,9},{9,8},{10,11... | collective-permute-start | bytes 786440 | tf_op jit(solution)/shard_map/ppermute | solution.py:106
